TPU v7x, 32 devices: a whole 2x2x4 slice. The times are simulated.
32 devices in a mesh: dp: 16 (over z, x, core), mp: 2 (over y).
Axes of the slice: x: 2, y: 2, z: 4, core: 2. Of those that a mesh axis runs over, the one named last changes fastest.
Arguments:
- tokens: bfloat16 [4096, 2560], P(('dp', 'mp')), may hold values from -6 to 6
- segments: int32 [4096], P('dp'), may hold values from 0 to 3, as said below
- positions: int32 [4096], P('dp'), may hold values from 0 to 511, as said below
- cotangent: bfloat16 [4096, 2560], P(('dp', 'mp')), may hold values from -6 to 6
- attn_gain: bfloat16 [2560], P(('dp', 'mp')), may hold values from 0.25 to 1.75
- ffn_gain: bfloat16 [2560], P(('dp', 'mp')), may hold values from 0.25 to 1.75
- w_kv: bfloat16 [2560, 512], P(('dp', 'mp')), may hold values from -0.125 to 0.125
- w_query: bfloat16 [2560, 2560], P('dp', 'mp'), may hold values from -0.25 to 0.25
- w_out: bfloat16 [2560, 2560], P('dp', 'mp'), may hold values from -0.5 to 0.5
- w_gate: bfloat16 [2560, 7680], P('dp', 'mp'), may hold values from -0.125 to 0.125
- w_up: bfloat16 [2560, 7680], P('dp', 'mp'), may hold values from -0.125 to 0.125
- w_down: bfloat16 [2560, 7680], P('dp', 'mp'), may hold values from -0.0625 to 0.0625
Outputs:
- mixed: bfloat16 [4096, 2560], P(('dp', 'mp'))
- tokens_grad: bfloat16 [4096, 2560], P(('dp', 'mp'))
- attn_gain_grad: float32 [2560], P(('dp', 'mp'))
- ffn_gain_grad: float32 [2560], P(('dp', 'mp'))
- w_kv_grad: float32 [2560, 512], P(('dp', 'mp'))
- w_query_grad: float32 [2560, 2560], P('dp', 'mp')
- w_out_grad: float32 [2560, 2560], P('dp', 'mp')
- w_gate_grad: float32 [2560, 7680], P('dp', 'mp')
- w_up_grad: float32 [2560, 7680], P('dp', 'mp')
- w_down_grad: float32 [2560, 7680], P('dp', 'mp')
Inputs may be any that keep to these rules, and one draw needn't show every extreme that they name: `segments`: within each sequence of 256 tokens the ids start at 0 and never fall; each id covers consecutive tokens. Inside a document positions rise by one from token to token; they start at 0 at every document that begins inside the sequence.
All inputs are finite; a program needn't handle non-finite values.
Results may differ from a plain program's by a relative error of at most 0.015.
Values may be sent and summed in bfloat16 or wider, within the bound.
A program may use at most 320 MiB of HBM per device.

v0:
```python
import functools

import jax
import jax.numpy as jnp
from jax import lax
from jax.experimental import pallas as pl
from jax.experimental.pallas import tpu as pltpu
from jax.sharding import PartitionSpec as P

WINDOW = 2048


epsilon = 1e-06
rope_base = 10000.0
masked_score = -1e30
VMEM_BYTES = 66_000_000


def norm_gain(values, gain):
    return values * lax.rsqrt(jnp.mean(values * values, axis=-1, keepdims=True) + epsilon) * gain


def rotary_angles(positions, head_width):
    quarter = head_width // 4
    freqs = rope_base ** (-jnp.arange(quarter).astype(jnp.float32) / quarter)
    phase = positions.astype(jnp.float32)[:, None] * freqs[None, :]
    return (jnp.cos(phase), jnp.sin(phase))


def rotate(values, cosine, sine):
    quarter = cosine.shape[-1]
    first_half = values[..., :quarter]
    second_half = values[..., quarter : 2 * quarter]
    return jnp.concatenate(
        [
            first_half * cosine - second_half * sine,
            second_half * cosine + first_half * sine,
            values[..., 2 * quarter :],
        ],
        axis=-1,
    )


def unrotate(values, cosine, sine):
    quarter = cosine.shape[-1]
    first_half = values[..., :quarter]
    second_half = values[..., quarter : 2 * quarter]
    return jnp.concatenate(
        [
            first_half * cosine + second_half * sine,
            second_half * cosine - first_half * sine,
            values[..., 2 * quarter :],
        ],
        axis=-1,
    )


def gelu_product(gate, up_proj):
    return jax.nn.gelu(gate, approximate=True) * up_proj


def matmul_nt(left, right):
    return lax.dot_general(
        left, right, (((1,), (1,)), ((), ())), preferred_element_type=jnp.float32
    )


def matmul_tn(left, right):
    return lax.dot_general(
        left, right, (((0,), (0,)), ((), ())), preferred_element_type=jnp.float32
    )


def block_allowed(segments, first_row, rows):
    seq_len = segments.shape[0]
    query_rows = first_row + jnp.arange(rows)
    key_rows = jnp.arange(seq_len)
    return (
        (segments[:, None] == segments[None, :])
        & (key_rows[None, :] <= query_rows[:, None])
        & (query_rows[:, None] - key_rows[None, :] < WINDOW)
    )


MESH_ID = pl.DeviceIdType.MESH
GELU_A = 0.7978845608028654
GELU_B = 0.044715
TILE = 256
WIDE = 512


def remote(src, dst, send_sem, recv_sem, where):
    return pltpu.make_async_remote_copy(
        src_ref=src,
        dst_ref=dst,
        send_sem=send_sem,
        recv_sem=recv_sem,
        device_id=where,
        device_id_type=MESH_ID,
    )


class Halves:
    def __init__(self, src, dst, send_sem, recv_sem, where):
        rows = src.shape[0] // 2
        cuts = [pl.ds(part * rows, rows) for part in range(2)]
        self.copies = [
            remote(src.at[cut], dst.at[cut], send_sem.at[part], recv_sem.at[part], where)
            for part, cut in enumerate(cuts)
        ]

    def start(self):
        for copy in self.copies:
            copy.start()

    def wait_recv(self):
        for copy in self.copies:
            copy.wait_recv()

    def wait_send(self):
        for copy in self.copies:
            copy.wait_send()


def dot_nn(left, right):
    return lax.dot_general(
        left, right, (((1,), (0,)), ((), ())), preferred_element_type=jnp.float32
    )


def gelu_parts(gate):
    square = gate * gate
    bend = jnp.tanh(GELU_A * gate * (1.0 + GELU_B * square))
    half = 0.5 * (1.0 + bend)
    slope = half + 0.5 * gate * (1.0 - bend * bend) * GELU_A * (1.0 + 3.0 * GELU_B * square)
    return gate * half, slope


def add_rows(first, rest, out, count):
    def body(index, carry):
        step = pl.ds(pl.multiple_of(index * 32, 32), 32)
        total = first[step, :].astype(jnp.float32)
        for other in rest:
            total = total + other[step, :].astype(jnp.float32)
        out[step, :] = total.astype(out.dtype)
        return carry

    lax.fori_loop(0, count // 32, body, 0)


def norm_back(values, gain, upstream):
    scale = lax.rsqrt(jnp.mean(values * values, axis=-1, keepdims=True) + epsilon)
    normed = values * scale
    pulled = gain * upstream
    back = scale * (pulled - normed * jnp.mean(normed * pulled, axis=-1, keepdims=True))
    return back, jnp.sum(upstream * normed, axis=0, keepdims=True)


def ffn_kernel(
    z_size,
    main,
    gain_ref,
    own_hbm,
    dy_hbm,
    w_hbm,
    mid_hbm,
    gm_ref,
    gain_part,
    mix_hbm,
    sums_hbm,
    gm_hbm,
    n2,
    dy,
    w3,
    h3,
    n2_t,
    dy_t,
    gn_part,
    mix_buf,
    gn_y,
    gn_z,
    gn_s,
    c_in,
    x_in,
    mid,
    load_sem,
    mix_sem,
    ag_y_send,
    ag_y_recv,
    ag_z_send,
    ag_z_recv,
    rs_y_send,
    rs_y_recv,
    rs_z_send,
    rs_z_recv,
    c_send,
    c_recv,
    x_send,
    x_recv,
    out_sem,
):
    own = own_hbm.shape[0] // 2
    width = own_hbm.shape[1]
    units = w3.shape[2]
    rows = c_in.shape[3]
    span = width // z_size
    me_y, me_z = lax.axis_index("mp"), lax.axis_index("z")
    me_x, me_c = lax.axis_index("x"), lax.axis_index("c")
    mine = pl.ds(pl.multiple_of(me_y * own, own), own)
    theirs = pl.ds(pl.multiple_of((1 - me_y) * own, own), own)
    to_y, to_x, to_c = {"mp": 1 - me_y}, {"x": 1 - me_x}, {"c": 1 - me_c}

    def ahead(step):
        return lax.rem(me_z + step, z_size)

    def to_z(step):
        return {"z": ahead(step)}

    def row_block(z_at, x_at, c_at):
        return pl.ds(pl.multiple_of(((z_at * 2 + x_at) * 2 + c_at) * rows, rows), rows)

    inner = (me_z > 0) & (me_z < z_size - 1)
    outer = (me_z == 0) | (me_z == z_size - 1)

    def w_load(index, columns):
        cols = pl.ds(0, columns)
        return pltpu.make_async_copy(
            w_hbm.at[index, :, cols], w3.at[index, :, cols], load_sem.at[z_size + index]
        )

    def w_loads(act):
        for case, columns in ((inner, units), (outer, main)):

            @pl.when(case)
            def _(columns=columns):
                for index in range(3):
                    act(w_load(index, columns))

    w_loads(lambda copy: copy.start())
    dy_loads = [
        pltpu.make_async_copy(dy_hbm.at[index], dy, load_sem.at[index])
        for index in range(z_size)
    ]
    own_load = pltpu.make_async_copy(own_hbm, n2.at[0], load_sem.at[z_size + 3])
    mid_load = pltpu.make_async_copy(mid_hbm, mid, load_sem.at[z_size + 4])
    for load in (own_load, dy_loads[0], mid_load):
        load.start()

    barrier = pltpu.get_barrier_semaphore()
    peers = [to_y, to_x, to_c] + [to_z(step) for step in range(1, z_size)]
    for where in peers:
        pl.semaphore_signal(barrier, inc=1, device_id=where, device_id_type=MESH_ID)
    pl.semaphore_wait(barrier, len(peers))

    def ag_y(index):
        block = n2.at[index, mine]
        return Halves(block, block, ag_y_send.at[index], ag_y_recv.at[index], to_y)

    def ag_y_in(index):
        block = n2.at[index, theirs]
        return Halves(block, block, ag_y_send.at[index], ag_y_recv.at[index], to_y)

    def ag_z(index):
        src = own_hbm.at[mine] if index == 0 else n2.at[index, mine]
        return Halves(
            src, n2.at[index + 1, mine], ag_z_send.at[index], ag_z_recv.at[index + 1], to_z(1)
        )

    def ag_z_in(index):
        block = n2.at[index, mine]
        return Halves(block, block, ag_z_send.at[0], ag_z_recv.at[index], to_z(1))

    def ag_last():
        return Halves(
            n2.at[2, theirs], n2.at[3, theirs], ag_y_send.at[3], ag_y_recv.at[3], to_z(1)
        )

    def forward(index):
        ag_z_in(index).wait_recv()
        ag_z(index).start()
        ag_y(index).start()

    ag_z(0).start()

    mix_copies = []

    def turn(source, target, index):
        def turn_tile(tile, carry):
            at = pl.ds(pl.multiple_of(tile * span, 128), span)
            target[at, pl.ds(index * 2 * own, 2 * own)] = source[:, at].T
            return carry

        lax.fori_loop(0, z_size, turn_tile, 0)

    def chunk(index):
        if index:
            mix_copies[index - 1].wait()
        dy_loads[index].wait()
        rows_at = pl.ds(index * 2 * own, 2 * own)

        def up_tile(tile, carry):
            cols = pl.ds(pl.multiple_of(tile * WIDE, WIDE), WIDE)
            gate = dot_nn(n2[index], w3[0, :, cols])
            up_proj = dot_nn(n2[index], w3[1, :, cols])
            grad_hidden = dot_nn(dy[...], w3[2, :, cols])
            act, slope = gelu_parts(gate)
            h3[0, rows_at, cols] = (grad_hidden * up_proj * slope).astype(jnp.bfloat16)
            h3[1, rows_at, cols] = (grad_hidden * act).astype(jnp.bfloat16)
            h3[2, rows_at, cols] = (act * up_proj).astype(jnp.bfloat16)
            return carry

        lax.fori_loop(0, units // WIDE, up_tile, 0)

        def down_tile(tile, carry):
            at = pl.ds(pl.multiple_of(tile * span, 128), span)
            normed = matmul_nt(w3[0, at, :], h3[0, rows_at, :]) + matmul_nt(
                w3[1, at, :], h3[1, rows_at, :]
            )
            mixed = matmul_nt(w3[2, at, :], h3[2, rows_at, :])
            for half in range(2):
                cols = slice(half * own, (half + 1) * own)
                gn_part[index, half, at, :] = normed[:, cols].astype(jnp.bfloat16)
                mix_buf[half, at, :] = mixed[:, cols].astype(jnp.bfloat16)
            return carry

        lax.fori_loop(0, z_size, down_tile, 0)
        copy = pltpu.make_async_copy(mix_buf, mix_hbm.at[index], mix_sem.at[index])
        copy.start()
        mix_copies.append(copy)
        if index:
            rs_y(index).start()
        turn(n2.at[index], n2_t, index)
        turn(dy, dy_t, index)
        if index + 1 < z_size:
            dy_loads[index + 1].start()

    def rs_y(index):
        return Halves(
            gn_part.at[index, 1 - me_y], gn_y.at[index], rs_y_send.at[index], rs_y_recv.at[index], to_y
        )

    def rs_z(index):
        return Halves(
            gn_s.at[index - 1],
            gn_z.at[index - 1],
            rs_z_send.at[index],
            rs_z_recv.at[index - 1],
            to_z(1),
        )

    def rs_step(index):
        rs_y(index).wait_recv()
        slot = (index - 2) % z_size
        if index != 1:
            Halves(
                gn_s.at[slot], gn_z.at[slot], rs_z_send.at[1], rs_z_recv.at[slot], to_z(1)
            ).wait_recv()

        def add_tile(tile, carry):
            at = pl.ds(pl.multiple_of(tile * TILE, TILE), TILE)
            total = gn_part[index, me_y, at, :].astype(jnp.float32) + gn_y[index, at, :].astype(
                jnp.float32
            )
            if index != 1:
                total = total + gn_z[slot, at, :].astype(jnp.float32)
            if index == 0:
                gm_ref[:, at] = total.T
            else:
                gn_s[index - 1, at, :] = total.astype(jnp.bfloat16)
            return carry

        lax.fori_loop(0, width // TILE, add_tile, 0)
        if index != 0:
            rs_z(index).start()


    def grads(step):
        at = pl.ds(pl.multiple_of(ahead(step) * span, 128), span)
        for kind, source in enumerate((n2_t, n2_t, dy_t)):

            def tile_body(tile, carry, kind=kind, source=source):
                cols = pl.ds(pl.multiple_of(tile * WIDE, WIDE), WIDE)
                w3[kind, at, cols] = dot_nn(source[at, :], h3[kind, :, cols]).astype(jnp.bfloat16)
                return carry

            lax.fori_loop(0, units // WIDE, tile_body, 0)
            for far in (1, 0):
                over_c(kind, step, far).start()

    def over_c(kind, step, far):
        x_at = 1 - me_x if far else me_x
        return remote(
            w3.at[kind, row_block(ahead(step), x_at, 1 - me_c)],
            c_in.at[kind, step, far],
            c_send.at[kind, step, far],
            c_recv.at[kind, step, far],
            to_c,
        )

    def over_x(kind):
        return remote(
            w3.at[kind, row_block(ahead(1), 1 - me_x, me_c)],
            x_in.at[kind],
            x_send.at[kind],
            x_recv.at[kind],
            to_x,
        )

    out_copies = []

    def keep(kind, step, far, block):
        copy = pltpu.make_async_copy(
            block, sums_hbm.at[kind, step, far], out_sem.at[kind, step, far]
        )
        copy.start()
        out_copies.append(copy)

    def core_sums(step):
        pairs = [(kind, far) for kind in range(3) for far in (1, 0)]
        if step == 1:
            pairs.sort(key=lambda pair: -pair[1])
        for kind, far in pairs:
            over_c(kind, step, far).wait_recv()
            x_at = 1 - me_x if far else me_x
            block = w3.at[kind, row_block(ahead(step), x_at, me_c)]
            add_rows(block, [c_in.at[kind, step, far]], block, rows)
            if step != 1:
                keep(kind, step, far, block)
            elif far:
                over_x(kind).start()

    def first_sums():
        for kind in range(3):
            over_x(kind).wait_recv()
            block = w3.at[kind, row_block(ahead(1), me_x, me_c)]
            add_rows(block, [x_in.at[kind]], block, rows)
            keep(kind, 1, 0, block)

    own_load.wait()
    w_loads(lambda copy: copy.wait())

    @pl.when(outer)
    def _():
        w3[:, :, main:] = jnp.zeros((3, width, units - main), jnp.bfloat16)

    chunk(0)
    forward(1)
    forward(2)
    ag_y_in(1).wait_recv()
    chunk(1)
    ag_y_in(2).wait_recv()
    ag_last().start()
    chunk(2)
    rs_step(1)
    ag_z_in(3).wait_recv()
    ag_last().wait_recv()
    chunk(3)
    rs_y(0).start()
    rs_step(2)
    grads(1)
    grads(2)
    core_sums(1)
    rs_step(3)
    grads(3)
    core_sums(2)
    grads(0)
    core_sums(3)
    rs_step(0)
    core_sums(0)

    cot_load = pltpu.make_async_copy(
        dy_hbm.at[0, mine], dy.at[pl.ds(0, own)], load_sem.at[z_size + 3]
    )
    cot_load.start()
    cot_load.wait()
    mid_load.wait()

    def mid_rows(index, total):
        at = pl.ds(pl.multiple_of(index * 32, 32), 32)
        grad, gain_sum = norm_back(mid[at, :], gain_ref[1:2, :], gm_ref[at, :])
        grad = grad + dy[at, :].astype(jnp.float32)
        gm_ref[at, :] = grad
        dy[pl.ds(pl.multiple_of(own + index * 32, 32), 32), :] = grad.astype(jnp.bfloat16)
        return total + gain_sum

    gain_sum = lax.fori_loop(0, own // 32, mid_rows, jnp.zeros((1, width), jnp.float32))
    gm_save = pltpu.make_async_copy(dy.at[pl.ds(own, own)], gm_hbm, load_sem.at[z_size + 3])
    gm_save.start()
    for index in range(4):
        gain_part[index : index + 1, :] = jnp.zeros((1, span), jnp.float32)
        gain_part[4 + index : 5 + index, :] = gain_sum[:, index * span : (index + 1) * span]
    first_sums()
    gm_save.wait()

    for copy in mix_copies[3:] + out_copies:
        copy.wait()
    for index in range(z_size):
        if index in (1, 2):
            ag_y(index).wait_send()
        if index == 3:
            ag_last().wait_send()
        rs_y(index).wait_send()
        if index < z_size - 1:
            ag_z(index).wait_send()
        if index:
            rs_z(index).wait_send()
        for kind in range(3):
            over_c(kind, index, 0).wait_send()
            over_c(kind, index, 1).wait_send()
            if index == 1:
                over_x(kind).wait_send()


def ffn_call(gains, normed, grad_all, weights, mid, rows, main):
    z_size = lax.axis_size("z")
    pair, width = normed.shape
    units = weights.shape[2]
    own = pair // 2
    wide = lambda *lead: pltpu.VMEM((*lead, width), jnp.bfloat16)
    tall = lambda *lead: pltpu.VMEM((*lead, width, own), jnp.bfloat16)
    dma = lambda *lead: pltpu.SemaphoreType.DMA(lead)
    vmem = pl.BlockSpec(memory_space=pltpu.VMEM)
    hbm = pl.BlockSpec(memory_space=pl.ANY)
    return pl.pallas_call(
        functools.partial(ffn_kernel, z_size, main),
        out_shape=(
            jax.ShapeDtypeStruct((own, width), jnp.float32),
            jax.ShapeDtypeStruct((8, width // z_size), jnp.float32),
            jax.ShapeDtypeStruct((z_size, 2, width, own), jnp.bfloat16),
            jax.ShapeDtypeStruct((3, z_size, 2, rows, units), jnp.bfloat16),
            jax.ShapeDtypeStruct((own, width), jnp.bfloat16),
        ),
        in_specs=[vmem, hbm, hbm, hbm, hbm],
        out_specs=(vmem, vmem, hbm, hbm, hbm),
        scratch_shapes=[
            wide(z_size, pair),
            wide(pair),
            pltpu.VMEM(weights.shape, jnp.bfloat16),
            pltpu.VMEM((3, z_size * pair, units), jnp.bfloat16),
            pltpu.VMEM((width, z_size * pair), jnp.bfloat16),
            pltpu.VMEM((width, z_size * pair), jnp.bfloat16),
            tall(z_size, 2),
            tall(2),
            tall(z_size),
            tall(z_size - 1),
            tall(z_size - 1),
            pltpu.VMEM((3, z_size, 2, rows, units), jnp.bfloat16),
            pltpu.VMEM((3, rows, units), jnp.bfloat16),
            pltpu.VMEM((own, width), jnp.float32),
            dma(z_size + 5),
            dma(z_size),
            dma(z_size, 2),
            dma(z_size, 2),
            dma(z_size, 2),
            dma(z_size, 2),
            dma(z_size, 2),
            dma(z_size, 2),
            dma(z_size, 2),
            dma(z_size, 2),
            dma(3, z_size, 2),
            dma(3, z_size, 2),
            dma(3),
            dma(3),
            dma(3, z_size, 2),
        ],
        compiler_params=pltpu.CompilerParams(
            collective_id=0, has_side_effects=True, vmem_limit_bytes=VMEM_BYTES
        ),
        cost_estimate=pl.CostEstimate(
            flops=18 * z_size * pair * width * units,
            bytes_accessed=4 * weights.size + 12 * z_size * pair * width,
            transcendentals=z_size * pair * units,
        ),
    )(gains, normed, grad_all, weights, mid)


def spin(values, table):
    first = values[:, : values.shape[1] // 2]
    turned = first * table[0] + pltpu.roll(first, first.shape[1] // 2, 1) * table[1]
    return jnp.concatenate([turned, values[:, values.shape[1] // 2 :]], axis=1)


def spin_back(values, table):
    first = values[:, : values.shape[1] // 2]
    turned = first * table[0] - pltpu.roll(first, first.shape[1] // 2, 1) * table[1]
    return jnp.concatenate([turned, values[:, values.shape[1] // 2 :]], axis=1)


def head_probs(rotated, keys, allowed):
    scores = jnp.where(allowed > 0.5, matmul_nt(rotated, keys), masked_score)
    weights = jnp.exp(scores - jnp.max(scores, axis=-1, keepdims=True))
    return weights / jnp.sum(weights, axis=-1, keepdims=True)


def ragged_split(columns, parts):
    main = columns // parts // 128 * 128
    return main, main + 128


def pre_kernel(
    z_size,
    tok_ref,
    wkv_ref,
    gain_one_ref,
    gain_two_ref,
    cos_ref,
    sin_ref,
    seg_ref,
    cot_hbm,
    wq_hbm,
    wo_hbm,
    wg_hbm,
    wu_hbm,
    wd_hbm,
    n1_ref,
    rot_ref,
    key_ref,
    val_ref,
    att_ref,
    mid_ref,
    n2_ref,
    gain_ref,
    allow_ref,
    kv_out,
    wq_out,
    wo_out,
    w3_out,
    dy_out,
    kv_w,
    q_w,
    o_w,
    tok,
    part,
    part_y,
    query,
    gain_rows,
    y_send,
    y_recv,
    ky_send,
    ky_recv,
    az_send,
    az_recv,
    ax_send,
    ax_recv,
    ac_send,
    ac_recv,
    fz_send,
    fz_recv,
    fx_send,
    fx_recv,
    fc_send,
    fc_recv,
    dz_send,
    dz_recv,
    dy_send,
    dy_recv,
    local_sem,
):
    me_z, me_x = lax.axis_index("z"), lax.axis_index("x")
    me_c, me_y = lax.axis_index("c"), lax.axis_index("mp")
    own, width = tok_ref.shape
    rows = wq_hbm.shape[0]
    half_rows = wkv_ref.shape[0]
    head = key_ref.shape[1]
    main, units = ragged_split(wg_hbm.shape[1], z_size)
    to_y, to_x, to_c = {"mp": 1 - me_y}, {"x": 1 - me_x}, {"c": 1 - me_c}

    def to_z(step):
        return {"z": lax.rem(me_z + step, z_size)}

    def from_z(step):
        return lax.rem(me_z - step + z_size, z_size)

    def row_block(step, x_at, c_at):
        start = ((from_z(step) * 2 + x_at) * 2 + c_at) * rows
        return pl.ds(pl.multiple_of(start, rows), rows)

    mine = pl.ds(pl.multiple_of(me_y * own, own), own)
    theirs = pl.ds(pl.multiple_of((1 - me_y) * own, own), own)
    bufs = (kv_w, q_w, o_w)
    inputs = (None, wq_hbm, wo_hbm)

    locals_ = []

    def local(src, dst):
        copy = pltpu.make_async_copy(src, dst, local_sem.at[len(locals_)])
        copy.start()
        locals_.append(copy)
        return copy

    here = row_block(0, me_x, me_c)
    own_q = local(wq_hbm, q_w.at[here])
    own_o = local(wo_hbm, o_w.at[here])
    ffn_in = (wg_hbm, wu_hbm, wd_hbm)

    def body_of(target):
        return pl.ds(pl.multiple_of(target * main, 128), main), pl.ds(0, main)

    def tail_of(target):
        start = z_size * main + lax.rem(target + 1, 2) * 128
        return pl.ds(pl.multiple_of(start, 128), 128), pl.ds(main, 128)

    def is_inner(at):
        return (at > 0) & (at < z_size - 1)

    own_f = []
    for kind in range(3):
        src, dst = body_of(me_z)
        own_f.append(local(ffn_in[kind].at[:, src], w3_out.at[kind, here, dst]))

    def own_tail(kind):
        src, dst = tail_of(me_z)
        return pltpu.make_async_copy(
            ffn_in[kind].at[:, src], w3_out.at[kind, here, dst], local_sem.at[12 + kind]
        )

    @pl.when(is_inner(me_z))
    def _():
        for kind in range(3):
            own_tail(kind).start()
    own_d = local(cot_hbm, dy_out.at[0, mine])

    kv_own = pl.ds(pl.multiple_of(here.start + me_y * half_rows, half_rows), half_rows)
    gain_rows[...] = jnp.zeros(gain_rows.shape, jnp.float32)
    gain_rows[0:1, :half_rows] = gain_one_ref[...].astype(jnp.float32)
    gain_rows[1:2, :half_rows] = gain_two_ref[...].astype(jnp.float32)
    spread = gain_rows[...].T
    kv_w[kv_own, : 2 * head] = wkv_ref[...]
    kv_w[kv_own, 2 * head :] = spread[:half_rows, :].astype(jnp.bfloat16)

    barrier = pltpu.get_barrier_semaphore()
    peers = [to_y, to_x, to_c] + [to_z(step) for step in range(1, z_size)]
    for where in peers:
        pl.semaphore_signal(barrier, inc=1, device_id=where, device_id_type=MESH_ID)
    pl.semaphore_wait(barrier, len(peers))

    tok_y = remote(tok_ref, tok.at[mine], y_send.at[1], y_recv.at[1], to_y)
    tok_y_in = remote(tok_ref, tok.at[theirs], y_send.at[1], y_recv.at[1], to_y)
    part_out = remote(part.at[theirs], part_y, y_send.at[2], y_recv.at[2], to_y)
    n2_y = remote(n2_ref.at[mine], n2_ref.at[mine], y_send.at[3], y_recv.at[3], to_y)
    n2_y_in = remote(n2_ref.at[theirs], n2_ref.at[theirs], y_send.at[3], y_recv.at[3], to_y)

    def block_of(kind, step, x_at):
        if kind:
            return row_block(step, x_at, me_c)
        return kv_rows(step, x_at, me_y)

    def kv_rows(step, x_at, y_at):
        start = row_block(step, x_at, me_c).start + y_at * half_rows
        return pl.ds(pl.multiple_of(start, half_rows), half_rows)

    def kv_y(step, far):
        x_at = 1 - me_x if far else me_x
        block = kv_w.at[kv_rows(step, x_at, me_y)]
        slot = step + z_size * far
        return remote(block, block, ky_send.at[slot], ky_recv.at[slot], to_y)

    def kv_y_in(step, far):
        x_at = 1 - me_x if far else me_x
        block = kv_w.at[kv_rows(step, x_at, 1 - me_y)]
        slot = step + z_size * far
        return remote(block, block, ky_send.at[slot], ky_recv.at[slot], to_y)

    def source(kind, step):
        if isinstance(step, int) and step == 0 and kind:
            return inputs[kind]
        return bufs[kind].at[block_of(kind, step, me_x)]

    first_z, last_z = (z_size - 1 - me_z) // (z_size - 1), me_z // (z_size - 1)
    inner = first_z + last_z == 0
    order = (0, 1 + 2 * first_z, 3 - first_z - last_z, 2 - first_z + last_z)
    hops = (
        None,
        (lax.rem(me_z + 1, z_size), 2),
        (lax.rem(me_z + z_size - 1, z_size), 2),
        (lax.rem(3 * (me_z + 3), z_size), lax.rem(2 * me_z + 3, z_size)),
    )

    def a_z_own(kind, right):
        return remote(
            source(kind, 0),
            bufs[kind].at[block_of(kind, 0, me_x)],
            az_send.at[kind, right],
            az_recv.at[kind, 1 if right else z_size - 1],
            to_z(1 if right else z_size - 1),
        )

    def a_z_start(kind):
        @pl.when(last_z == 0)
        def _():
            a_z_own(kind, 1).start()

        @pl.when(first_z == 0)
        def _():
            a_z_own(kind, 0).start()

    def a_z(kind, index):
        target, slot = hops[index]
        block = bufs[kind].at[block_of(kind, order[index], me_x)]
        return remote(
            block, block, az_send.at[kind, 1 + index], az_recv.at[kind, slot], {"z": target}
        )

    def a_z_next(kind, index):
        @pl.when(inner)
        def _():
            a_z(kind, index).start()

    def a_z_done(kind):
        @pl.when(last_z == 0)
        def _():
            a_z_own(kind, 1).wait_send()

        @pl.when(first_z == 0)
        def _():
            a_z_own(kind, 0).wait_send()

        @pl.when(inner)
        def _():
            for index in range(1, z_size):
                a_z(kind, index).wait_send()

    def a_z_in(kind, step):
        block = bufs[kind].at[block_of(kind, step, me_x)]
        return remote(block, block, az_send.at[kind, 0], az_recv.at[kind, step], to_z(1))

    def a_x(kind, step):
        return remote(
            source(kind, step),
            bufs[kind].at[block_of(kind, step, me_x)],
            ax_send.at[kind, step],
            ax_recv.at[kind, step],
            to_x,
        )

    def a_x_in(kind, step):
        block = bufs[kind].at[block_of(kind, step, 1 - me_x)]
        return remote(block, block, ax_send.at[kind, step], ax_recv.at[kind, step], to_x)

    def a_c(kind, step, far):
        x_at = 1 - me_x if far else me_x
        block = bufs[kind].at[row_block(step, x_at, me_c)]
        src = source(kind, step) if kind and not far else block
        slot = step + z_size * far
        return remote(src, block, ac_send.at[kind, slot], ac_recv.at[kind, slot], to_c)

    def a_c_in(kind, step, far):
        x_at = 1 - me_x if far else me_x
        block = bufs[kind].at[row_block(step, x_at, 1 - me_c)]
        slot = step + z_size * far
        return remote(block, block, ac_send.at[kind, slot], ac_recv.at[kind, slot], to_c)

    def f_z(kind, step, act):
        target = lax.rem(me_z + step, z_size)

        def piece(index, src, dst):
            return remote(
                ffn_in[kind].at[:, src],
                w3_out.at[kind, here, dst],
                fz_send.at[kind, step, index],
                fz_recv.at[kind, step, index],
                to_z(step),
            )

        act(piece(0, *body_of(target)))

        @pl.when(is_inner(target))
        def _():
            act(piece(1, *tail_of(target)))

    def f_z_wait(kind, step):
        block = row_block(step, me_x, me_c)

        def piece(index, dst):
            part = w3_out.at[kind, block, dst]
            return remote(
                part, part, fz_send.at[kind, step, index], fz_recv.at[kind, step, index], to_z(step)
            )

        piece(0, pl.ds(0, main)).wait_recv()

        @pl.when(inner)
        def _():
            piece(1, pl.ds(main, 128)).wait_recv()

    def f_x(kind, step, x_at, act):
        for case, columns in ((inner, units), (first_z + last_z > 0, main)):

            @pl.when(case)
            def _(columns=columns):
                block = w3_out.at[kind, row_block(step, x_at, me_c), pl.ds(0, columns)]
                act(remote(block, block, fx_send.at[kind, step], fx_recv.at[kind, step], to_x))

    def f_x_start(kind, step):
        f_x(kind, step, me_x, lambda copy: copy.start())

    def f_x_wait(kind, step):
        f_x(kind, step, 1 - me_x, lambda copy: copy.wait_recv())

    def f_x_done(kind, step):
        f_x(kind, step, me_x, lambda copy: copy.wait_send())

    def f_c(kind, step, far):
        block = w3_out.at[kind, row_block(step, 1 - me_x if far else me_x, me_c)]
        slot = step + z_size * far
        return remote(block, block, fc_send.at[kind, slot], fc_recv.at[kind, slot], to_c)

    def f_c_in(kind, step, far):
        block = w3_out.at[kind, row_block(step, 1 - me_x if far else me_x, 1 - me_c)]
        slot = step + z_size * far
        return remote(block, block, fc_send.at[kind, slot], fc_recv.at[kind, slot], to_c)

    def d_source(step):
        return cot_hbm if isinstance(step, int) else dy_out.at[step, mine]

    def d_z_own(right):
        slot = 1 if right else z_size - 1
        return remote(
            cot_hbm, dy_out.at[slot, mine], dz_send.at[right], dz_recv.at[slot], to_z(slot)
        )

    def d_z_start():
        @pl.when(last_z == 0)
        def _():
            d_z_own(1).start()

        @pl.when(first_z == 0)
        def _():
            d_z_own(0).start()

    def d_z(index):
        target, slot = hops[index]
        return remote(
            dy_out.at[order[index], mine],
            dy_out.at[slot, mine],
            dz_send.at[1 + index],
            dz_recv.at[slot],
            {"z": target},
        )

    def d_z_done():
        @pl.when(last_z == 0)
        def _():
            d_z_own(1).wait_send()

        @pl.when(first_z == 0)
        def _():
            d_z_own(0).wait_send()

        @pl.when(inner)
        def _():
            for index in range(1, z_size):
                d_z(index).wait_send()

    def d_z_in(step):
        block = dy_out.at[step, mine]
        return remote(block, block, dz_send.at[0], dz_recv.at[step], to_z(1))

    def d_y(step):
        return remote(
            d_source(step), dy_out.at[step, mine], dy_send.at[step], dy_recv.at[step], to_y
        )

    def d_y_in(step):
        block = dy_out.at[step, theirs]
        return remote(block, block, dy_send.at[step], dy_recv.at[step], to_y)

    for kind in (1, 0, 2):
        a_z_start(kind)
        a_x(kind, 0).start()
    kv_y(0, 0).start()
    tok_y.start()
    for kind in (1, 2):
        a_c(kind, 0, 0).start()

    for at_end, away in ((first_z, 1), (last_z, z_size - 1)):

        @pl.when(at_end > 0)
        def _(away=away):
            for kind in range(3):
                f_z(kind, away, lambda copy: copy.start())

    tok[mine, :] = tok_ref[...]
    seq = 2 * own
    query_at = lax.broadcasted_iota(jnp.int32, (seq, seq), 0)
    key_at = lax.broadcasted_iota(jnp.int32, (seq, seq), 1)
    segment = seg_ref[...].astype(jnp.float32)
    same = jnp.broadcast_to(segment, (8, seq)).T[:, :1] == segment
    allowed = same & (key_at <= query_at) & (query_at - key_at < WINDOW)
    allow_ref[...] = jnp.where(allowed, 1.0, 0.0)
    d_y(0).start()

    def from_x(index):
        step = order[index]
        for kind in (1, 0, 2):
            a_x_in(kind, step).wait_recv()
            if kind:
                a_c(kind, step, 1).start()
            else:
                kv_y(step, 1).start()

    def from_y(index):
        step = order[index]
        for far in range(2):
            kv_y_in(step, far).wait_recv()
            a_c(0, step, far).start()

    for index in range(1, z_size):
        step = order[index]
        for kind in (1, 0, 2):
            a_z_in(kind, step).wait_recv()
            a_z_next(kind, index)
            a_x(kind, step).start()
            if kind:
                a_c(kind, step, 0).start()
            else:
                kv_y(step, 0).start()
        if index == z_size - 2:
            d_z_start()
        if index == z_size - 1:
            for copy in own_f:
                copy.wait()

            @pl.when(inner)
            def _():
                for kind in range(3):
                    own_tail(kind).wait()

            for kind in range(3):
                for away, sent in ((1, first_z), (3, last_z), (2, 0)):

                    @pl.when(sent == 0 if away != 2 else me_z >= 0)
                    def _(kind=kind, away=away):
                        f_z(kind, away, lambda copy: copy.start())

            for kind in range(3):
                f_x_start(kind, 0)
                f_c(kind, 0, 0).start()
        if index >= 2:
            from_x(index - 2)
            from_y(index - 2)
    for index in (z_size - 2, z_size - 1):
        from_x(index)
        from_y(index)

    def hand_on(kind, step):
        f_z_wait(kind, step)
        f_x_start(kind, step)
        f_c(kind, step, 0).start()

    def cross(kind, step):
        f_x_wait(kind, step)
        f_c(kind, step, 1).start()

    def pass_cotangent(step):
        d_z_in(order[step]).wait_recv()

        @pl.when(inner)
        def _():
            d_z(step).start()

        d_y(order[step]).start()

    def pass_if(case, step):
        @pl.when(case)
        def _():
            pass_cotangent(step)

    outer = first_z + last_z > 0
    tok_y_in.wait_recv()
    own_q.wait()
    own_o.wait()
    for kind in (0, 1):
        for step in range(z_size):
            for far in range(2):
                a_c_in(kind, step, far).wait_recv()

    gains = kv_w[:, 2 * head :].astype(jnp.float32).T[:8, :]
    gain_ref[...] = gains

    def norm_rows(index, carry):
        at = pl.ds(pl.multiple_of(index * 32, 32), 32)
        values = tok[at, :].astype(jnp.float32)
        scale = lax.rsqrt(jnp.mean(values * values, axis=-1, keepdims=True) + epsilon)
        n1_ref[at, :] = (values * scale * gain_ref[0:1, :]).astype(jnp.bfloat16)
        return carry

    lax.fori_loop(0, 2 * own // 32, norm_rows, 0)
    hand_on(0, order[1])
    table = (cos_ref[...], sin_ref[...])
    key_ref[...] = spin(dot_nn(n1_ref[...], kv_w[:, :head]), table).astype(jnp.bfloat16)
    val_ref[...] = dot_nn(n1_ref[...], kv_w[:, head : 2 * head]).astype(jnp.bfloat16)
    hand_on(0, order[2])
    head_scale = head ** (-0.5)
    heads = att_ref.shape[1] // head

    half_cols = att_ref.shape[1] // 2
    for index in range(2):
        cols = pl.ds(index * half_cols, half_cols)
        query[:, cols] = dot_nn(n1_ref[...], q_w[:, cols])

    def attend(index):
        cols = pl.ds(index * head, head)
        rotated = (spin(query[:, cols], table) * head_scale).astype(jnp.bfloat16)
        rot_ref[:, cols] = rotated
        probs = head_probs(rotated, key_ref[...], allow_ref[...]).astype(jnp.bfloat16)
        att_ref[:, cols] = dot_nn(probs, val_ref[...]).astype(jnp.bfloat16)

    tasks = [
        lambda: (pass_cotangent(1), pass_if(inner, 2)),
        lambda: hand_on(0, order[3]),
        lambda: (cross(0, 0), hand_on(1, order[1])),
        lambda: cross(1, 0),
        lambda: (cross(2, 0), hand_on(1, order[2])),
    ]
    for index in range(heads):
        attend(index)
        if index < len(tasks):
            tasks[index]()
    for step in range(z_size):
        for far in range(2):
            a_c_in(2, step, far).wait_recv()
    saves = [
        local(kv_w, kv_out),
        local(q_w, wq_out),
        local(o_w, wo_out),
    ]
    span = width // 4

    def project(index, carry):
        cols = pl.ds(pl.multiple_of(index * span, span), span)
        part[:, cols] = matmul_nt(att_ref[...], o_w[cols, :]).astype(jnp.bfloat16)
        return carry

    lax.fori_loop(0, 4, project, 0)
    part_out.start()
    hand_on(1, order[3])
    pass_if(outer, 2)
    pass_if(inner, 3)
    cross(0, order[1])
    hand_on(2, order[1])
    part_out.wait_recv()

    def middle(index, carry):
        at = pl.ds(pl.multiple_of(index * 32, 32), 32)
        there = pl.ds(pl.multiple_of(me_y * own + index * 32, 32), 32)
        values = (
            tok_ref[at, :].astype(jnp.float32)
            + part[there, :].astype(jnp.float32)
            + part_y[at, :].astype(jnp.float32)
        )
        mid_ref[at, :] = values
        scale = lax.rsqrt(jnp.mean(values * values, axis=-1, keepdims=True) + epsilon)
        n2_ref[there, :] = (values * scale * gain_ref[1:2, :]).astype(jnp.bfloat16)
        return carry

    lax.fori_loop(0, own // 32, middle, 0)
    n2_y.start()
    hand_on(2, order[2])
    cross(0, order[2])
    cross(0, order[3])
    hand_on(2, order[3])
    pass_if(outer, 3)
    for kind in (1, 2):
        for index in (1, 2, 3):
            cross(kind, order[index])
    for kind in range(3):
        for step in range(z_size):
            for far in range(2):
                f_c_in(kind, step, far).wait_recv()
    for step in range(z_size):
        d_y_in(step).wait_recv()
    n2_y_in.wait_recv()

    for kind in range(3):
        a_z_done(kind)
    d_z_done()
    tok_y.wait_send()
    part_out.wait_send()
    n2_y.wait_send()
    own_d.wait()
    for copy in saves:
        copy.wait()
    for step in range(z_size):
        d_y(step).wait_send()
        for far in range(2):
            kv_y(step, far).wait_send()
        for kind in range(3):
            if step:
                f_z(kind, step, lambda copy: copy.wait_send())
            a_x(kind, step).wait_send()
            f_x_done(kind, step)
            for far in range(2):
                a_c(kind, step, far).wait_send()
                f_c(kind, step, far).wait_send()


def pre_call(
    tokens, w_kv, gain_one, gain_two, table, segments, cotangent, w_query, w_out, ffn
):
    z_size = lax.axis_size("z")
    own, width = tokens.shape
    seq = 2 * own
    rows, cols = w_query.shape
    head = table[0].shape[1] * 2
    units = ragged_split(ffn[0].shape[1], z_size)[1]
    low = lambda *dims: jax.ShapeDtypeStruct(dims, jnp.bfloat16)
    full = lambda *dims: jax.ShapeDtypeStruct(dims, jnp.float32)
    dma = lambda *lead: pltpu.SemaphoreType.DMA(lead)
    vmem = pl.BlockSpec(memory_space=pltpu.VMEM)
    hbm = pl.BlockSpec(memory_space=pl.ANY)
    wide = lambda *lead: pltpu.VMEM((*lead, width), jnp.bfloat16)
    return pl.pallas_call(
        functools.partial(pre_kernel, z_size),
        out_shape=(
            low(seq, width),
            low(seq, cols),
            low(seq, head),
            low(seq, head),
            low(seq, cols),
            full(own, width),
            low(seq, width),
            full(8, width),
            full(seq, seq),
            low(width, 2 * head + 128),
            low(width, cols),
            low(width, cols),
            low(3, width, units),
            low(z_size, seq, width),
        ),
        in_specs=[vmem] * 7 + [hbm] * 6,
        out_specs=(vmem,) * 9 + (hbm,) * 5,
        scratch_shapes=[
            pltpu.VMEM((width, 2 * head + 128), jnp.bfloat16),
            pltpu.VMEM((width, cols), jnp.bfloat16),
            pltpu.VMEM((width, cols), jnp.bfloat16),
            wide(seq),
            wide(seq),
            wide(own),
            pltpu.VMEM((seq, cols), jnp.float32),
            pltpu.VMEM((128, 128), jnp.float32),
            dma(4),
            dma(4),
            dma(2 * z_size),
            dma(2 * z_size),
            dma(3, z_size + 1),
            dma(3, z_size),
            dma(3, z_size),
            dma(3, z_size),
            dma(3, 2 * z_size),
            dma(3, 2 * z_size),
            dma(3, z_size, 2),
            dma(3, z_size, 2),
            dma(3, z_size),
            dma(3, z_size),
            dma(3, 2 * z_size),
            dma(3, 2 * z_size),
            dma(z_size + 1),
            dma(z_size),
            dma(z_size),
            dma(z_size),
            dma(16),
        ],
        compiler_params=pltpu.CompilerParams(
            collective_id=1, has_side_effects=True, vmem_limit_bytes=VMEM_BYTES
        ),
        cost_estimate=pl.CostEstimate(
            flops=8 * seq * width * cols,
            bytes_accessed=8 * width * (cols + units),
            transcendentals=seq * seq * cols // head,
        ),
    )(tokens, w_kv, gain_one, gain_two, *table, segments, cotangent, w_query, w_out, *ffn)


def post_kernel(
    z_size,
    main,
    tok_ref,
    gain_ref,
    gain_part_ref,
    n1_ref,
    rot_ref,
    key_ref,
    val_ref,
    att_ref,
    cos_ref,
    sin_ref,
    allow_ref,
    kv_hbm,
    wq_hbm,
    wo_hbm,
    mix_hbm,
    gmf_hbm,
    gmb_hbm,
    mid_hbm,
    sums_hbm,
    mixed_ref,
    tgrad_ref,
    gsum_ref,
    kvg_ref,
    qg_ref,
    og_ref,
    ffn_out,
    kv_w,
    q_w,
    o_w,
    o_part,
    gm,
    gm_f,
    gq,
    gkv,
    kv_sum,
    back_y,
    mix_y,
    mix_z,
    mix_s,
    o_c,
    o_x,
    o_z,
    q_c,
    q_x,
    q_z,
    kv_y,
    kv_c,
    kv_x,
    kv_z,
    gain_own,
    gain_in,
    ffn_in,
    ffn_own,
    load_sem,
    own_sem,
    fx_send,
    fx_recv,
    fz_send,
    fz_recv,
    y_send,
    y_recv,
    my_send,
    my_recv,
    mz_send,
    mz_recv,
    wc_send,
    wc_recv,
    wx_send,
    wx_recv,
    wz_send,
    wz_recv,
    kc_send,
    kc_recv,
    kz_send,
    kz_recv,
    g_send,
    g_recv,
):
    me_z, me_x = lax.axis_index("z"), lax.axis_index("x")
    me_c, me_y = lax.axis_index("c"), lax.axis_index("mp")
    own, width = tok_ref.shape
    seq = 2 * own
    head = key_ref.shape[1]
    cols_here = att_ref.shape[1]
    heads = cols_here // head
    rows = qg_ref.shape[0]
    span = width // z_size
    mine = pl.ds(pl.multiple_of(me_y * own, own), own)
    theirs = pl.ds(pl.multiple_of((1 - me_y) * own, own), own)
    to_y, to_x, to_c = {"mp": 1 - me_y}, {"x": 1 - me_x}, {"c": 1 - me_c}
    head_scale = head ** (-0.5)

    def behind(step):
        return lax.rem(me_z - step + z_size, z_size)

    def to_z(step):
        return {"z": lax.rem(me_z + step, z_size)}

    def row_block(step, x_at, c_at):
        start = ((behind(step) * 2 + x_at) * 2 + c_at) * rows
        return pl.ds(pl.multiple_of(start, rows), rows)

    loads = [
        pltpu.make_async_copy(wo_hbm, o_w, load_sem.at[0]),
        pltpu.make_async_copy(wq_hbm, q_w, load_sem.at[1]),
        pltpu.make_async_copy(
            kv_hbm.at[:, :, :, :, :, pl.ds(0, 2 * head)], kv_w, load_sem.at[2]
        ),
    ]
    for step in range(z_size):
        loads.append(
            pltpu.make_async_copy(mix_hbm.at[step, me_y], mix_s.at[step], load_sem.at[3 + step])
        )
    loads.append(pltpu.make_async_copy(gmf_hbm, gm_f, load_sem.at[3 + z_size]))
    loads.append(pltpu.make_async_copy(gmb_hbm, gm.at[mine], load_sem.at[4 + z_size]))
    mid_load = pltpu.make_async_copy(mid_hbm, gm_f, load_sem.at[5 + z_size])
    for load in loads:
        load.start()

    barrier = pltpu.get_barrier_semaphore()
    peers = [to_y, to_x, to_c] + [to_z(step) for step in range(1, z_size)]
    for where in peers:
        pl.semaphore_signal(barrier, inc=1, device_id=where, device_id_type=MESH_ID)
    pl.semaphore_wait(barrier, len(peers))

    tasks = [(step, kind) for step in (2, 3) for kind in range(3)]

    def f_x(index):
        step, kind = tasks[index]
        return remote(
            sums_hbm.at[kind, step, 1],
            ffn_in.at[index],
            fx_send.at[index],
            fx_recv.at[index],
            to_x,
        )

    def f_own(index):
        step, kind = tasks[index]
        return pltpu.make_async_copy(
            sums_hbm.at[kind, step, 0], ffn_own.at[index % 2], own_sem.at[index % 2]
        )

    def f_z(step, kind, source_z, act):
        for case, columns in (
            ((source_z > 0) & (source_z < z_size - 1), ffn_out.shape[3]),
            ((source_z == 0) | (source_z == z_size - 1), main),
        ):

            @pl.when(case)
            def _(columns=columns):
                cols = pl.ds(0, columns)
                if step == 1:
                    src = sums_hbm.at[kind, 1, 0, :, cols]
                else:
                    src = ffn_in.at[tasks.index((step, kind)), :, cols]
                act(
                    remote(
                        src,
                        ffn_out.at[kind, step, :, cols],
                        fz_send.at[kind, step],
                        fz_recv.at[kind, step],
                        to_z(step),
                    )
                )

    def tick(index):
        step, kind = tasks[index]
        f_x(index).wait_recv()
        f_own(index).wait()
        block = ffn_in.at[index]
        add_rows(block, [ffn_own.at[index % 2]], block, rows)
        if index + 2 < len(tasks):
            f_own(index + 2).start()
        f_z(step, kind, me_z, lambda copy: copy.start())

    def f_x_own(kind):
        return remote(
            sums_hbm.at[kind, 0, 1],
            ffn_out.at[kind, 0],
            fx_send.at[len(tasks) + kind],
            fx_recv.at[len(tasks) + kind],
            to_x,
        )

    f_own(0).start()
    f_own(1).start()
    for index in range(len(tasks)):
        f_x(index).start()
    for kind in range(3):
        f_z(1, kind, me_z, lambda copy: copy.start())

    gm_y = remote(gmb_hbm, gm.at[mine], y_send.at[0], y_recv.at[0], to_y)
    gm_y_in = remote(gm.at[theirs], gm.at[theirs], y_send.at[0], y_recv.at[0], to_y)
    gm_y.start()

    first_z, last_z = (z_size - 1 - me_z) // (z_size - 1), me_z // (z_size - 1)
    inner = first_z + last_z == 0
    order = (
        0,
        1 + (me_z + 1) // 2,
        2 + (2 * me_z - 3) * (1 - first_z - last_z),
        3 - 2 * (me_z // 2),
    )
    right = (None, 1 - me_z // 2, (3 - me_z) * (2 - me_z) // 6 + me_z // 2 * (1 - last_z), 1 - me_z // 2)

    def hop_slot(index):
        step, way = order[index], right[index]
        return way * lax.rem(step + 1, z_size) + (1 - way) * (step - 1 + 4 * ((3 - step) // 2))

    def hop_target(index):
        return {"z": me_z + 2 * right[index] - 1}

    def mix_over_y(step):
        return remote(
            mix_hbm.at[step, 1 - me_y], mix_y.at[step], my_send.at[step], my_recv.at[step], to_y
        )

    def mix_over_z(index):
        slot = hop_slot(index)
        return remote(
            mix_s.at[order[index]],
            mix_z.at[slot],
            mz_send.at[index],
            mz_recv.at[slot],
            hop_target(index),
        )

    def mix_z_in(slot):
        return remote(mix_z.at[slot], mix_z.at[slot], mz_send.at[1], mz_recv.at[slot], to_z(1))

    def mix_add(step, others, last):
        def add_tile(tile, carry):
            at = pl.ds(pl.multiple_of(tile * TILE, TILE), TILE)
            total = mix_s[step, at, :].astype(jnp.float32)
            for other in others:
                total = total + other[at, :].astype(jnp.float32)
            if last:
                mixed_ref[:, at] = (gm_f[:, at] + total.T).astype(jnp.bfloat16)
            else:
                mix_s[step, at, :] = total.astype(jnp.bfloat16)
            return carry

        lax.fori_loop(0, width // TILE, add_tile, 0)

    def mix_step(index):
        step = order[index]
        mix_over_y(step).wait_recv()
        from_y = mix_y.at[step]
        if index:

            @pl.when(inner)
            def _():
                mix_z_in(step).wait_recv()
                mix_add(step, [from_y, mix_z.at[step]], False)

            @pl.when(first_z + last_z > 0)
            def _():
                mix_add(step, [from_y], False)

            mix_over_z(index).start()
        else:
            mid_load.wait()

            @pl.when(first_z == 0)
            def _():
                mix_z_in(0).wait_recv()

            @pl.when(last_z == 0)
            def _():
                mix_z_in(z_size).wait_recv()

            @pl.when(inner)
            def _():
                mix_add(0, [from_y, mix_z.at[0], mix_z.at[z_size]], True)

            @pl.when(first_z > 0)
            def _():
                mix_add(0, [from_y, mix_z.at[z_size]], True)

            @pl.when(last_z > 0)
            def _():
                mix_add(0, [from_y, mix_z.at[0]], True)

    for index in (1, 2, 3, 0):
        mix_over_y(order[index]).start()

    kinds = ((o_part, o_c, o_x, o_z, og_ref), (o_w, q_c, q_x, q_z, qg_ref))

    def w_c(kind, step, far):
        x_at = 1 - me_x if far else me_x
        return remote(
            kinds[kind][0].at[row_block(step, x_at, 1 - me_c)],
            kinds[kind][1].at[step, far],
            wc_send.at[kind, step, far],
            wc_recv.at[kind, step, far],
            to_c,
        )

    def w_x(kind, step):
        return remote(
            kinds[kind][0].at[row_block(step, 1 - me_x, me_c)],
            kinds[kind][2].at[step],
            wx_send.at[kind, step],
            wx_recv.at[kind, step],
            to_x,
        )

    def w_z(kind, index):
        step, slot = order[index], hop_slot(index)
        return remote(
            kinds[kind][0].at[row_block(step, me_x, me_c)],
            kinds[kind][3].at[slot],
            wz_send.at[kind, index],
            wz_recv.at[kind, slot],
            hop_target(index),
        )

    def w_z_in(kind, slot):
        block = kinds[kind][3].at[slot]
        return remote(block, block, wz_send.at[kind, 1], wz_recv.at[kind, slot], to_z(1))

    def w_x_stage(kind, index):
        step = order[index]
        w_c(kind, step, 1).wait_recv()
        block = kinds[kind][0].at[row_block(step, 1 - me_x, me_c)]
        add_rows(block, [kinds[kind][1].at[step, 1]], block, rows)
        w_x(kind, step).start()

    def w_z_stage(kind, index):
        part, from_c, from_x, from_z, result = kinds[kind]
        step = order[index]
        w_c(kind, step, 0).wait_recv()
        w_x(kind, step).wait_recv()
        block = part.at[row_block(step, me_x, me_c)]
        others = [from_c.at[step, 0], from_x.at[step]]
        if index:

            @pl.when(inner)
            def _():
                w_z_in(kind, step).wait_recv()
                add_rows(block, [*others, from_z.at[step]], block, rows)

            @pl.when(first_z + last_z > 0)
            def _():
                add_rows(block, others, block, rows)

            w_z(kind, index).start()
        else:

            @pl.when(first_z == 0)
            def _():
                w_z_in(kind, 0).wait_recv()

            @pl.when(last_z == 0)
            def _():
                w_z_in(kind, z_size).wait_recv()

            @pl.when(inner)
            def _():
                add_rows(block, [*others, from_z.at[0], from_z.at[z_size]], result, rows)

            @pl.when(first_z > 0)
            def _():
                add_rows(block, [*others, from_z.at[z_size]], result, rows)

            @pl.when(last_z > 0)
            def _():
                add_rows(block, [*others, from_z.at[0]], result, rows)

    def w_product(kind, index, left, values):
        step = order[index]
        at = pl.ds(pl.multiple_of(behind(step) * span, 128), span)
        turned = left[:, at].T

        def tile_body(tile, carry):
            cols = pl.ds(pl.multiple_of(tile * TILE, TILE), TILE)
            kinds[kind][0][at, cols] = dot_nn(turned, values[:, cols]).astype(jnp.bfloat16)
            return carry

        lax.fori_loop(0, cols_here // TILE, tile_body, 0)
        for far in (1, 0):
            w_c(kind, step, far).start()

    tick(0)
    tick(1)
    loads[-1].wait()
    gm_y_in.wait_recv()
    w_product(0, 1, gm, att_ref)
    w_product(0, 2, gm, att_ref)
    w_x_stage(0, 1)
    w_product(0, 3, gm, att_ref)
    w_x_stage(0, 2)
    tick(2)
    w_product(0, 0, gm, att_ref)
    w_x_stage(0, 3)
    for load in loads[:-1]:
        load.wait()

    kv_sum[...] = jnp.zeros(kv_sum.shape, jnp.float32)
    table = (cos_ref[...], sin_ref[...])

    for index in range(2):
        cols = pl.ds(index * (cols_here // 2), cols_here // 2)
        gq[:, cols] = dot_nn(gm[...], o_w[:, cols]).astype(jnp.bfloat16)

    def attend_back(index):
        cols = pl.ds(index * head, head)
        grad_vals = gq[:, cols]
        rotated = rot_ref[:, cols]
        probs = head_probs(rotated, key_ref[...], allow_ref[...])
        grad_probs = matmul_nt(grad_vals, val_ref[...])
        delta = jnp.sum(probs * grad_probs, axis=-1, keepdims=True)
        grad_scores = (probs * (grad_probs - delta)).astype(jnp.bfloat16)
        grad_rot = dot_nn(grad_scores, key_ref[...])
        gq[:, cols] = (spin_back(grad_rot, table) * head_scale).astype(jnp.bfloat16)
        kv_sum[0] += matmul_tn(grad_scores, rotated)
        kv_sum[1] += matmul_tn(probs.astype(jnp.bfloat16), grad_vals)

    for index in range(heads):
        attend_back(index)
        if index == 0:
            w_x_stage(0, 0)
        if 3 + index < len(tasks):
            tick(3 + index)
        if index == heads - 1:
            mix_step(1)
    gkv[:, :head] = spin_back(kv_sum[0], table).astype(jnp.bfloat16)
    gkv[:, head:] = kv_sum[1].astype(jnp.bfloat16)

    w_product(1, 1, n1_ref, gq)
    w_product(1, 2, n1_ref, gq)
    w_x_stage(1, 1)
    w_z_stage(0, 1)
    w_product(1, 3, n1_ref, gq)
    w_x_stage(1, 2)
    w_product(1, 0, n1_ref, gq)
    w_x_stage(1, 3)
    w_x_stage(1, 0)
    for kind in range(3):
        f_x_own(kind).start()

    gm_y.wait_send()
    back = gm
    def input_tile(index, carry):
        at = pl.ds(pl.multiple_of(index * span, 128), span)
        back[:, at] = (
            matmul_nt(gq[...], q_w[at, :]) + matmul_nt(gkv[...], kv_w[index].reshape(span, 2 * head))
        ).astype(jnp.bfloat16)
        return carry

    lax.fori_loop(0, z_size, input_tile, 0)
    back_out = remote(back.at[theirs], back_y, y_send.at[1], y_recv.at[1], to_y)
    back_out.start()

    kv_part = kv_w

    def kv_tile(index, carry):
        at = pl.ds(pl.multiple_of(index * span, 128), span)
        product = dot_nn(n1_ref[:, at].T, gkv[...]).astype(jnp.bfloat16)
        kv_part[index] = product.reshape(kv_part.shape[1:])
        return carry

    lax.fori_loop(0, z_size, kv_tile, 0)
    kv_over_y = remote(kv_part.at[:, :, :, 1 - me_y], kv_y, y_send.at[2], y_recv.at[2], to_y)
    kv_over_y.start()
    mix_step(2)
    w_z_stage(0, 2)
    mix_step(3)
    w_z_stage(0, 3)

    back_out.wait_recv()

    def input_rows(index, total):
        at = pl.ds(pl.multiple_of(index * 32, 32), 32)
        there = pl.ds(pl.multiple_of(me_y * own + index * 32, 32), 32)
        upstream = back[there, :].astype(jnp.float32) + back_y[at, :].astype(jnp.float32)
        grad, gain_part = norm_back(
            tok_ref[at, :].astype(jnp.float32), gain_ref[0:1, :], upstream
        )
        tgrad_ref[at, :] = (gm_f[at, :] + grad).astype(jnp.bfloat16)
        return total + gain_part

    attn_gain_part = lax.fori_loop(
        0, own // 32, input_rows, jnp.zeros((1, width), jnp.float32)
    )
    for index in range(4):
        at = slice(index * span, (index + 1) * span)
        gain_own[0, index : index + 1, :] = attn_gain_part[:, at]
        gain_own[0, 4 + index : 5 + index, :] = gain_part_ref[4 + index : 5 + index, :]

    def gain_send(stage, where):
        return remote(
            gain_own.at[stage], gain_in.at[stage], g_send.at[stage], g_recv.at[stage], where
        )

    gain_hops = [gain_send(0, to_y), gain_send(1, to_c), gain_send(2, to_x)]
    gain_last = [
        remote(
            gain_own.at[3], gain_in.at[2 + step], g_send.at[2 + step], g_recv.at[2 + step], to_z(step)
        )
        for step in range(1, z_size)
    ]

    def gain_fold(stage):
        gain_hops[stage].wait_recv()
        gain_own[stage + 1] = gain_own[stage] + gain_in[stage]

    gain_hops[0].start()
    mid_load.start()
    w_z_stage(1, 1)
    w_z_stage(0, 0)
    w_z_stage(1, 2)
    gain_fold(0)
    gain_hops[1].start()
    mix_step(0)
    w_z_stage(1, 3)
    gain_fold(1)
    gain_hops[2].start()
    kv_over_y.wait_recv()

    def kv_add_y(index, carry):
        for x_at in range(2):
            for c_at in range(2):
                block = kv_part.at[index, x_at, c_at, me_y]
                block[...] = (
                    block[...].astype(jnp.float32) + kv_y[index, x_at, c_at].astype(jnp.float32)
                ).astype(jnp.bfloat16)
        return carry

    lax.fori_loop(0, z_size, kv_add_y, 0)
    kv_over_c = remote(
        kv_part.at[:, :, 1 - me_c, me_y], kv_c, kc_send.at[0], kc_recv.at[0], to_c
    )
    kv_over_c.start()
    gain_fold(2)
    for copy in gain_last:
        copy.start()
    kv_over_c.wait_recv()

    def kv_add_c(index, carry):
        for x_at in range(2):
            block = kv_part.at[index, x_at, me_c, me_y]
            block[...] = (
                block[...].astype(jnp.float32) + kv_c[index, x_at].astype(jnp.float32)
            ).astype(jnp.bfloat16)
        return carry

    lax.fori_loop(0, z_size, kv_add_c, 0)
    kv_over_x = remote(
        kv_part.at[:, 1 - me_x, me_c, me_y], kv_x, kc_send.at[1], kc_recv.at[1], to_x
    )
    kv_over_x.start()
    w_z_stage(1, 0)
    kv_over_x.wait_recv()

    def kv_add_x(index, carry):
        block = kv_part.at[index, me_x, me_c, me_y]
        block[...] = (
            block[...].astype(jnp.float32) + kv_x[index].astype(jnp.float32)
        ).astype(jnp.bfloat16)
        return carry

    lax.fori_loop(0, z_size, kv_add_x, 0)
    kv_over_z = [
        remote(
            kv_part.at[lax.rem(me_z + step, z_size), me_x, me_c, me_y],
            kv_z.at[step - 1],
            kz_send.at[step],
            kz_recv.at[step],
            to_z(step),
        )
        for step in range(1, z_size)
    ]
    for copy in kv_over_z:
        copy.start()
    for copy in gain_last:
        copy.wait_recv()
    gsum_ref[...] = gain_own[3] + gain_in[3] + gain_in[4] + gain_in[5]
    for copy in kv_over_z:
        copy.wait_recv()
    kvg_ref[...] = (
        kv_part[me_z, me_x, me_c, me_y].astype(jnp.float32)
        + kv_z[0].astype(jnp.float32)
        + kv_z[1].astype(jnp.float32)
        + kv_z[2].astype(jnp.float32)
    )

    back_out.wait_send()
    kv_over_y.wait_send()
    kv_over_c.wait_send()
    kv_over_x.wait_send()
    for kind in range(3):
        f_x_own(kind).wait()
    for index in range(len(tasks)):
        f_x(index).wait_send()
    for step in range(1, z_size):
        for kind in range(3):
            f_z(step, kind, me_z, lambda copy: copy.wait_send())
            f_z(step, kind, behind(step), lambda copy: copy.wait_recv())
    for copy in gain_hops + gain_last + kv_over_z:
        copy.wait_send()
    for step in range(z_size):
        mix_over_y(step).wait_send()
        if step:
            mix_over_z(step).wait_send()
        for kind in range(2):
            w_c(kind, step, 0).wait_send()
            w_c(kind, step, 1).wait_send()
            w_x(kind, step).wait_send()
            if step:
                w_z(kind, step).wait_send()


def post_call(
    tokens,
    gains,
    gain_part,
    normed_one,
    rotated,
    keys,
    values,
    attn_vals,
    table,
    allowed,
    kv_weight,
    query_weight,
    out_weight,
    mix_parts,
    grad_mid,
    grad_mid_low,
    mid,
    ffn_sums,
    main,
):
    z_size = lax.axis_size("z")
    own, width = tokens.shape
    seq = 2 * own
    head = keys.shape[1]
    cols = attn_vals.shape[1]
    rows = width // (4 * z_size)
    units = ffn_sums.shape[4]
    low = lambda *dims: pltpu.VMEM(dims, jnp.bfloat16)
    full = lambda *dims: pltpu.VMEM(dims, jnp.float32)
    out_full = lambda *dims: jax.ShapeDtypeStruct(dims, jnp.float32)
    out_low = lambda *dims: jax.ShapeDtypeStruct(dims, jnp.bfloat16)
    dma = lambda *lead: pltpu.SemaphoreType.DMA(lead)
    vmem = pl.BlockSpec(memory_space=pltpu.VMEM)
    hbm = pl.BlockSpec(memory_space=pl.ANY)
    z = z_size
    return pl.pallas_call(
        functools.partial(post_kernel, z_size, main),
        out_shape=(
            out_low(own, width),
            out_low(own, width),
            out_full(8, width // z),
            out_full(rows // 2, 2 * head),
            out_full(rows, cols),
            out_full(rows, cols),
            out_low(3, z, rows, units),
        ),
        in_specs=[vmem] * 11 + [hbm] * 8,
        out_specs=(vmem,) * 6 + (hbm,),
        scratch_shapes=[
            low(z, 2, 2, 2, rows // 2, 2 * head),
            low(width, cols),
            low(width, cols),
            low(width, cols),
            low(seq, width),
            full(own, width),
            low(seq, cols),
            low(seq, 2 * head),
            full(2, seq, head),
            low(own, width),
            low(z, width, own),
            low(z + 1, width, own),
            low(z, width, own),
            low(z, 2, rows, cols),
            low(z, rows, cols),
            low(z + 1, rows, cols),
            low(z, 2, rows, cols),
            low(z, rows, cols),
            low(z + 1, rows, cols),
            low(z, 2, 2, rows // 2, 2 * head),
            low(z, 2, rows // 2, 2 * head),
            low(z, rows // 2, 2 * head),
            low(z - 1, rows // 2, 2 * head),
            full(4, 8, width // z),
            full(6, 8, width // z),
            low(6, rows, units),
            low(2, rows, units),
            dma(6 + z),
            dma(2),
            dma(9),
            dma(9),
            dma(3, z),
            dma(3, z),
            dma(3),
            dma(3),
            dma(z),
            dma(z),
            dma(z),
            dma(z + 1),
            dma(2, z, 2),
            dma(2, z, 2),
            dma(2, z),
            dma(2, z),
            dma(2, z),
            dma(2, z + 1),
            dma(2),
            dma(2),
            dma(z),
            dma(z),
            dma(6),
            dma(6),
        ],
        compiler_params=pltpu.CompilerParams(
            collective_id=2, has_side_effects=True, vmem_limit_bytes=VMEM_BYTES
        ),
        cost_estimate=pl.CostEstimate(
            flops=14 * seq * width * cols,
            bytes_accessed=10 * width * cols,
            transcendentals=seq * seq * cols // head,
        ),
    )(
        tokens,
        gains,
        gain_part,
        normed_one,
        rotated,
        keys,
        values,
        attn_vals,
        *table,
        allowed,
        kv_weight.reshape(z, 2, 2, 2, rows // 2, kv_weight.shape[1]),
        query_weight,
        out_weight,
        mix_parts,
        grad_mid,
        grad_mid_low,
        mid,
        ffn_sums,
    )


def layout_kernel(
    z_size,
    main,
    sum_ref,
    ffn_ref,
    q_ref,
    o_ref,
    kv_ref,
    mixed_in,
    tgrad_in,
    wg_ref,
    wu_ref,
    wd_ref,
    qg_ref,
    og_ref,
    kvg_ref,
    mixed_ref,
    tgrad_ref,
):
    me_z = lax.axis_index("z")
    for kind, out in enumerate((wg_ref, wu_ref, wd_ref)):
        for step in range(z_size):
            at = lax.rem(me_z - step + z_size, z_size)
            values = ffn_ref[kind, step].astype(jnp.float32)
            if step == 0:
                values = values + sum_ref[kind, 0, 0].astype(jnp.float32)
            body = pl.ds(pl.multiple_of(at * main, 128), main)
            out[:, body] = values[:, :main]

            @pl.when((at > 0) & (at < z_size - 1))
            def _(out=out, at=at, values=values):
                tail = z_size * main + lax.rem(at + 1, 2) * 128
                out[:, pl.ds(pl.multiple_of(tail, 128), 128)] = values[:, main:]
    qg_ref[...] = q_ref[...]
    og_ref[...] = o_ref[...]
    kvg_ref[...] = kv_ref[...]
    mixed_ref[...] = mixed_in[...]
    tgrad_ref[...] = tgrad_in[...]


def layout_call(ffn_sums, ffn_grads, query_grad, out_grad, kv_grad, mixed, tokens_grad, ffn_cols):
    z_size = lax.axis_size("z")
    main, units = ragged_split(ffn_cols, z_size)
    rows, cols = query_grad.shape
    parts = rows // 32
    kv_rows = kv_grad.shape[0] // parts
    full = lambda *dims: jax.ShapeDtypeStruct(dims, jnp.float32)
    row = lambda height, width: pl.BlockSpec((height, width), lambda index: (index, 0))
    own, width = mixed.shape
    share = pl.BlockSpec((own, width // parts), lambda index: (0, index))
    specs = [row(32, cols), row(32, cols), row(kv_rows, kv_grad.shape[1]), share, share]
    return pl.pallas_call(
        functools.partial(layout_kernel, z_size, main),
        grid=(parts,),
        out_shape=(
            *[full(rows, ffn_cols)] * 3,
            full(rows, cols),
            full(rows, cols),
            full(*kv_grad.shape),
            jax.ShapeDtypeStruct(mixed.shape, jnp.bfloat16),
            jax.ShapeDtypeStruct(mixed.shape, jnp.bfloat16),
        ),
        in_specs=[
            pl.BlockSpec((3, 1, 1, 32, units), lambda index: (0, 0, 0, index, 0)),
            pl.BlockSpec((3, z_size, 32, units), lambda index: (0, 0, index, 0)),
            *specs,
        ],
        out_specs=(*[row(32, ffn_cols)] * 3, *specs),
        compiler_params=pltpu.CompilerParams(vmem_limit_bytes=VMEM_BYTES),
    )(ffn_sums, ffn_grads, query_grad, out_grad, kv_grad, mixed, tokens_grad)


FF_SPLIT = 4


def ffn_pass(normed, grad_out, gate_weight, up_weight, down_weight):
    gate = jnp.dot(normed, gate_weight, preferred_element_type=jnp.float32)
    up_proj = jnp.dot(normed, up_weight, preferred_element_type=jnp.float32)
    grad_hidden = jnp.dot(grad_out, down_weight, preferred_element_type=jnp.float32)
    product, pull = jax.vjp(gelu_product, gate, up_proj)
    hidden = product.astype(jnp.bfloat16)
    grad_gate_f, grad_up_f = pull(grad_hidden)
    grad_gate = grad_gate_f.astype(jnp.bfloat16)
    grad_up = grad_up_f.astype(jnp.bfloat16)
    mixed_part = matmul_nt(hidden, down_weight).astype(jnp.bfloat16)
    normed_part = (matmul_nt(grad_gate, gate_weight) + matmul_nt(grad_up, up_weight)).astype(
        jnp.bfloat16
    )
    weight_parts = [
        matmul_tn(normed, grad_gate).astype(jnp.bfloat16),
        matmul_tn(normed, grad_up).astype(jnp.bfloat16),
        matmul_tn(grad_out, hidden).astype(jnp.bfloat16),
    ]
    return mixed_part, normed_part, weight_parts


def shards_general(
    tokens,
    segments,
    positions,
    cotangent,
    attn_gain,
    ffn_gain,
    w_kv,
    w_query,
    w_out,
    w_gate,
    w_up,
    w_down,
):
    everywhere = ("z", "xc", "mp")
    dp = ("z", "xc")
    z_size = lax.axis_size("z")
    xc_size = lax.axis_size("xc")
    gains = lax.all_gather(
        jnp.stack([attn_gain, ffn_gain], axis=1), everywhere, axis=0, tiled=True
    ).astype(jnp.float32)
    gain_one, gain_two = gains[:, 0], gains[:, 1]
    kv_weight = lax.all_gather(w_kv, everywhere, axis=0, tiled=True)
    head_dim = kv_weight.shape[1] // 2
    width = tokens.shape[1]
    seq_len = segments.shape[0]
    heads_here = w_query.shape[1] // head_dim
    scale = head_dim ** (-0.5)
    cosine, sine = rotary_angles(positions, head_dim)
    inputs_f = tokens.astype(jnp.float32)
    tokens_all = lax.all_gather(tokens, "mp", axis=0, tiled=True)
    normed_one = norm_gain(tokens_all.astype(jnp.float32), gain_one).astype(jnp.bfloat16)
    query_weight = lax.all_gather(w_query, dp, axis=0, tiled=True)
    out_weight = lax.all_gather(w_out, dp, axis=0, tiled=True)

    rows = w_gate.shape[0]
    unit = w_gate.shape[1] // z_size

    def spread(weight):
        pieces = weight.reshape(rows, z_size, unit).transpose(1, 0, 2)
        pieces = lax.all_to_all(pieces, "z", split_axis=0, concat_axis=0, tiled=True)
        return lax.all_gather(pieces, "xc", axis=1, tiled=False).reshape(width, unit)

    gate_weight, up_weight, down_weight = spread(w_gate), spread(w_up), spread(w_down)
    grad_all = lax.all_gather(cotangent, ("z", "mp"), axis=0, tiled=True)

    query = jnp.dot(normed_one, query_weight, preferred_element_type=jnp.float32).reshape(
        seq_len, heads_here, head_dim
    )
    rotated = (rotate(query, cosine[:, None], sine[:, None]) * scale).astype(jnp.bfloat16)
    keyval = jnp.dot(normed_one, kv_weight, preferred_element_type=jnp.float32)
    keys = rotate(keyval[:, :head_dim], cosine, sine).astype(jnp.bfloat16)
    values = keyval[:, head_dim:].astype(jnp.bfloat16)
    allowed = block_allowed(segments, 0, seq_len)
    scores = jnp.einsum("thd,sd->hts", rotated, keys, preferred_element_type=jnp.float32)
    scores = jnp.where(allowed[None], scores, masked_score)
    row_max = jnp.max(scores, axis=-1, keepdims=True)
    weights = jnp.exp(scores - row_max)
    probs = weights / jnp.sum(weights, axis=-1, keepdims=True)
    probs_low = probs.astype(jnp.bfloat16)
    attn_vals = (
        jnp.einsum("hts,sd->thd", probs_low, values, preferred_element_type=jnp.float32)
        .reshape(seq_len, heads_here * head_dim)
        .astype(jnp.bfloat16)
    )
    mid = inputs_f + lax.psum_scatter(
        matmul_nt(attn_vals, out_weight).astype(jnp.bfloat16),
        "mp",
        scatter_dimension=0,
        tiled=True,
    ).astype(jnp.float32)
    normed_two = norm_gain(mid, gain_two).astype(jnp.bfloat16)
    normed_all = lax.all_gather(normed_two, ("z", "mp"), axis=0, tiled=True)

    mixed_part, normed_part, weight_parts = ffn_pass(
        normed_all, grad_all, gate_weight, up_weight, down_weight
    )
    grad_normed_two = lax.psum_scatter(
        normed_part, ("z", "mp"), scatter_dimension=0, tiled=True
    ).astype(jnp.float32)
    mixed = (
        mid
        + lax.psum_scatter(mixed_part, ("z", "mp"), scatter_dimension=0, tiled=True).astype(
            jnp.float32
        )
    ).astype(jnp.bfloat16)

    def collect(part):
        pieces = part.reshape(z_size, xc_size, rows, unit).transpose(1, 0, 2, 3)
        pieces = pieces.reshape(xc_size * z_size * rows, unit)
        pieces = lax.psum_scatter(pieces, "xc", scatter_dimension=0, tiled=True)
        pieces = pieces.reshape(z_size, rows, unit)
        pieces = lax.all_to_all(pieces, "z", split_axis=0, concat_axis=0, tiled=True)
        return pieces.transpose(1, 0, 2).reshape(rows, z_size * unit).astype(jnp.float32)

    w_gate_grad, w_up_grad, w_down_grad = [collect(part) for part in weight_parts]

    norm_pull_two = jax.vjp(norm_gain, mid, gain_two)[1]
    grad_mid_norm, grad_gain_two = norm_pull_two(grad_normed_two)
    grad_mid = cotangent.astype(jnp.float32) + grad_mid_norm
    grad_mid_all = lax.all_gather(grad_mid.astype(jnp.bfloat16), "mp", axis=0, tiled=True)
    grad_vals = (
        jnp.dot(grad_mid_all, out_weight, preferred_element_type=jnp.float32)
        .astype(jnp.bfloat16)
        .reshape(seq_len, heads_here, head_dim)
    )
    grad_probs = jnp.einsum("thd,sd->hts", grad_vals, values, preferred_element_type=jnp.float32)
    delta = jnp.sum(probs * grad_probs, axis=-1, keepdims=True)
    grad_scores = (probs * (grad_probs - delta)).astype(jnp.bfloat16)
    grad_rot = jnp.einsum("hts,sd->thd", grad_scores, keys, preferred_element_type=jnp.float32)
    key_sum = jnp.einsum("hts,thd->sd", grad_scores, rotated, preferred_element_type=jnp.float32)
    value_sum = jnp.einsum("hts,thd->sd", probs_low, grad_vals, preferred_element_type=jnp.float32)
    grad_query = (
        (unrotate(grad_rot, cosine[:, None], sine[:, None]) * scale)
        .reshape(seq_len, heads_here * head_dim)
        .astype(jnp.bfloat16)
    )
    grad_kv = jnp.concatenate([unrotate(key_sum, cosine, sine), value_sum], axis=1).astype(
        jnp.bfloat16
    )
    grad_normed_one = lax.psum_scatter(
        (matmul_nt(grad_query, query_weight) + matmul_nt(grad_kv, kv_weight)).astype(jnp.bfloat16),
        "mp",
        scatter_dimension=0,
        tiled=True,
    ).astype(jnp.float32)
    norm_pull_one = jax.vjp(norm_gain, inputs_f, gain_one)[1]
    grad_input_norm, grad_gain_one = norm_pull_one(grad_normed_one)
    tokens_grad = (grad_mid + grad_input_norm).astype(jnp.bfloat16)

    w_query_grad = lax.psum_scatter(
        matmul_tn(normed_one, grad_query).astype(jnp.bfloat16), dp, scatter_dimension=0, tiled=True
    ).astype(jnp.float32)
    w_out_grad = lax.psum_scatter(
        matmul_tn(grad_mid_all, attn_vals).astype(jnp.bfloat16), dp, scatter_dimension=0, tiled=True
    ).astype(jnp.float32)
    small = jnp.concatenate(
        [matmul_tn(normed_one, grad_kv), grad_gain_one[:, None], grad_gain_two[:, None]], axis=1
    )
    small = lax.psum_scatter(small, everywhere, scatter_dimension=0, tiled=True)
    kv_grad = small[:, : 2 * head_dim]
    return (
        mixed,
        tokens_grad,
        small[:, 2 * head_dim],
        small[:, 2 * head_dim + 1],
        kv_grad,
        w_query_grad,
        w_out_grad,
        w_gate_grad,
        w_up_grad,
        w_down_grad,
    )


def shards_fast(
    tokens,
    segments,
    positions,
    cotangent,
    attn_gain,
    ffn_gain,
    w_kv,
    w_query,
    w_out,
    w_gate,
    w_up,
    w_down,
):
    quarter = w_kv.shape[1] // 8
    lane = jnp.arange(2 * quarter)
    freqs = rope_base ** (-(lane % quarter).astype(jnp.float32) / quarter)
    phase = positions.astype(jnp.float32)[:, None] * freqs[None, :]
    table = (jnp.cos(phase), jnp.where(lane < quarter, -1.0, 1.0)[None, :] * jnp.sin(phase))
    (
        normed_one,
        rotated,
        keys,
        values,
        attn_vals,
        mid,
        normed_two,
        gains,
        allowed,
        kv_weight,
        query_weight,
        out_weight,
        ffn_weights,
        grad_all,
    ) = pre_call(
        tokens,
        w_kv,
        attn_gain[None, :],
        ffn_gain[None, :],
        table,
        segments[None, :],
        cotangent,
        w_query,
        w_out,
        (w_gate, w_up, w_down),
    )
    main = ragged_split(w_gate.shape[1], lax.axis_size("z"))[0]
    grad_mid, gain_part, mix_parts, ffn_sums, grad_mid_low = ffn_call(
        gains, normed_two, grad_all, ffn_weights, mid, w_gate.shape[0], main
    )
    mixed, tokens_grad, gain_grads, kv_grad, query_grad, out_grad, ffn_grads = post_call(
        tokens,
        gains,
        gain_part,
        normed_one,
        rotated,
        keys,
        values,
        attn_vals,
        table,
        allowed,
        kv_weight,
        query_weight,
        out_weight,
        mix_parts,
        grad_mid,
        grad_mid_low,
        mid,
        ffn_sums,
        main,
    )
    *ffn_out, query_grad, out_grad, kv_grad, mixed, tokens_grad = layout_call(
        ffn_sums,
        ffn_grads,
        query_grad,
        out_grad,
        kv_grad,
        mixed,
        tokens_grad,
        w_gate.shape[1],
    )
    share = attn_gain.shape[0]
    place = lax.axis_index(("z", "x", "c", "mp")) * share
    gain_grads = gain_grads.reshape(2, gain_grads.size // 2)
    gain_grads = lax.dynamic_slice(gain_grads, (0, place), (2, share))
    return (
        mixed,
        tokens_grad,
        gain_grads[0],
        gain_grads[1],
        kv_grad,
        query_grad,
        out_grad,
        *ffn_out,
    )


def solution(mesh):
    dp_size, mp_size = mesh.shape["dp"], mesh.shape["mp"]
    if dp_size == 4 * FF_SPLIT and mp_size == 2:
        body, dp = shards_fast, ("z", "x", "c")
        sizes = (FF_SPLIT, 2, 2, mp_size)
    else:
        body, dp = shards_general, ("z", "xc")
        sizes = (FF_SPLIT, dp_size // FF_SPLIT, mp_size)
    all_axes = (*dp, "mp")
    fine = jax.sharding.Mesh(mesh.devices.reshape(sizes), all_axes)
    in_specs = (
        P(all_axes, None),
        P(dp),
        P(dp),
        P(all_axes, None),
        P(all_axes),
        P(all_axes),
        P(all_axes, None),
        P(dp, "mp"),
        P(dp, "mp"),
        P(dp, "mp"),
        P(dp, "mp"),
        P(dp, "mp"),
    )
    out_specs = (
        P(all_axes, None),
        P(all_axes, None),
        P(all_axes),
        P(all_axes),
        P(all_axes, None),
        P(dp, "mp"),
        P(dp, "mp"),
        P(dp, "mp"),
        P(dp, "mp"),
        P(dp, "mp"),
    )
    return jax.shard_map(body, mesh=fine, in_specs=in_specs, out_specs=out_specs, check_vma=False)
```

profile of v0, /device:TPU:0, one launch (start us, length us, event | category | flops | bytes accessed | tf_op | source)
XLA Modules:
  0.0 493.4 jit_solution(4046483003538580904)
XLA Ops:
  0.7 0.7 convert_element_type.10
  1.3 1.2 fusion
  2.6 198.9 %shard_map.195 = (bf16[256,2560]{1,0:T(8,128)(2,1)}, bf16[256,1280]{1,0:T(8,128)(2,1)}, bf16[256,256]{1,0:T(8,128)(2,1)}, bf16[256,256]{1,0:T(8,128)(2,1)}, bf16...) custom-call(bf16[128,2560]{1,0:T(8,128)(2,1)} %tok_ref.3, ...), custom_call_target="tpu_custom_call" | custom-call | flops 6710886400 | bytes 47185920 | tf_op jit(solution)/shard_map/pallas_call | solution.py:1213
  201.5 112.0 %shard_map.196 = (f32[128,2560]{1,0:T(8,128)}, f32[8,640]{1,0:T(8,128)}, bf16[4,2,2560,128]{3,2,1,0:T(8,128)(2,1)}, bf16[3,4,2,160,1024]{4,3,2,1,0:T(8,128)(2,1)}, bf16[128,2560]{1,0:T(8,128)(2,1)}) custom-call(f32[8,2560]{1,0:T(8,128)} %get-tuple-element.44.gain_ref, bf16[256,2560]{1,0:T(8,128)(2,1)} %get-tuple-element.45.own_hbm, ...), custom_call_target="tpu_custom_call" | custom-call | flops 48318382080 | bytes 62914560 | tf_op jit(solution)/shard_map/pallas_call | solution.py:524
  313.5 170.2 %shard_map.197 = (bf16[128,2560]{1,0:T(8,128)(2,1)}, bf16[128,2560]{1,0:T(8,128)(2,1)}, f32[8,640]{1,0:T(8,128)}, f32[80,512]{1,0:T(8,128)}, f32[160,1280]{1,0:T...) custom-call(bf16[128,2560]{1,0:T(8,128)(2,1)} %tok_ref.3, f32[8,2560]{1,0:T(8,128)} %get-tuple-element.44.gain_ref, ...), custom_call_target="tpu_custom_call" | custom-call | flops 11744051200 | bytes 32768000 | tf_op jit(solution)/shard_map/pallas_call | solution.py:1928
  483.7 0.0 copy-start
  483.7 8.7 %shard_map.198 = (f32[160,3840]{1,0:T(8,128)}, f32[160,3840]{1,0:T(8,128)}, f32[160,3840]{1,0:T(8,128)}, f32[160,1280]{1,0:T(8,128)}, f32[160,1280]{1,0:T(8,128)...) custom-call(bf16[3,4,2,160,1024]{4,3,2,1,0:T(8,128)(2,1)} %get-tuple-element.49.sums_hbm.sum_ref, ...), custom_call_target="tpu_custom_call" | custom-call | tf_op jit(solution)/shard_map/pallas_call | solution.py:2075
  492.4 0.0 copy-done
  492.4 0.1 constant_dynamic-slice_fusion
  492.5 0.5 slice_bitcast_fusion
  (2 shorter events, 0.0 us)
Async XLA Ops:
  483.7 8.7 %copy-start = (f32[8,640]{1,0:T(8,128)S(1)}, f32[8,640]{1,0:T(8,128)}, u32[]{:S(2)}) copy-start(f32[8,640]{1,0:T(8,128)} %get-tuple-element.71) | copy-start | bytes 61444
where the time goes:
time: 500 us; the launch traced here: 493 us
  Pallas kernels  490 us (98%)
    pallas_call x1, Pallas kernels, pre_call(): pl.pallas_call(functools.partial(pre_kernel, z_size), out_shape=(low(seq,...  199 us
    pallas_call x1, Pallas kernels, post_call(): pl.pallas_call(functools.partial(post_kernel, z_size, main), out_shape=(o...  170 us
    pallas_call x1, Pallas kernels, ffn_call(): pl.pallas_call(functools.partial(ffn_kernel, z_size, main), out_shape=(ja...  112 us

commit v1 on v0

--- a/solution.py
+++ b/solution.py
@@ -1026,12 +1026,13 @@
                 for kind in range(3):
                     own_tail(kind).wait()
 
-            for kind in range(3):
-                for away, sent in ((1, first_z), (3, last_z), (2, 0)):
-
-                    @pl.when(sent == 0 if away != 2 else me_z >= 0)
-                    def _(kind=kind, away=away):
-                        f_z(kind, away, lambda copy: copy.start())
+            for at, ways in enumerate(((3, 2), (3, 2, 1), (1, 2, 3), (1, 2))):
+
+                @pl.when(me_z == at)
+                def _(ways=ways):
+                    for kind in range(3):
+                        for away in ways:
+                            f_z(kind, away, lambda copy: copy.start())
 
             for kind in range(3):
                 f_x_start(kind, 0)
@@ -2065,13 +2066,13 @@
     z_size = lax.axis_size("z")
     main, units = ragged_split(ffn_cols, z_size)
     rows, cols = query_grad.shape
-    parts = rows // 32
+    parts = rows // 80
     kv_rows = kv_grad.shape[0] // parts
     full = lambda *dims: jax.ShapeDtypeStruct(dims, jnp.float32)
     row = lambda height, width: pl.BlockSpec((height, width), lambda index: (index, 0))
     own, width = mixed.shape
     share = pl.BlockSpec((own, width // parts), lambda index: (0, index))
-    specs = [row(32, cols), row(32, cols), row(kv_rows, kv_grad.shape[1]), share, share]
+    specs = [row(80, cols), row(80, cols), row(kv_rows, kv_grad.shape[1]), share, share]
     return pl.pallas_call(
         functools.partial(layout_kernel, z_size, main),
         grid=(parts,),
@@ -2084,11 +2085,11 @@
             jax.ShapeDtypeStruct(mixed.shape, jnp.bfloat16),
         ),
         in_specs=[
-            pl.BlockSpec((3, 1, 1, 32, units), lambda index: (0, 0, 0, index, 0)),
-            pl.BlockSpec((3, z_size, 32, units), lambda index: (0, 0, index, 0)),
+            pl.BlockSpec((3, 1, 1, 80, units), lambda index: (0, 0, 0, index, 0)),
+            pl.BlockSpec((3, z_size, 80, units), lambda index: (0, 0, index, 0)),
             *specs,
         ],
-        out_specs=(*[row(32, ffn_cols)] * 3, *specs),
+        out_specs=(*[row(80, ffn_cols)] * 3, *specs),
         compiler_params=pltpu.CompilerParams(vmem_limit_bytes=VMEM_BYTES),
     )(ffn_sums, ffn_grads, query_grad, out_grad, kv_grad, mixed, tokens_grad)
 

time: 500 us -> 505 us (1.010)
  no operation moved by 1% of the time
where the time goes in v1:
time: 505 us; the launch traced here: 498 us
  Pallas kernels  495 us (98%)
    pallas_call x1, Pallas kernels, pre_call(): pl.pallas_call(functools.partial(pre_kernel, z_size), out_shape=(low(seq,...  203 us
    pallas_call x1, Pallas kernels, post_call(): pl.pallas_call(functools.partial(post_kernel, z_size, main), out_shape=(o...  170 us
    pallas_call x1, Pallas kernels, ffn_call(): pl.pallas_call(functools.partial(ffn_kernel, z_size, main), out_shape=(ja...  115 us

profile of v1, /device:TPU:0, one launch (start us, length us, event | category | flops | bytes accessed | tf_op | source)
XLA Modules:
  0.0 498.3 jit_solution(6047854620032379220)
XLA Ops:
  0.7 0.7 convert_element_type.10
  1.3 1.2 fusion
  2.6 202.8 %shard_map.195 = (bf16[256,2560]{1,0:T(8,128)(2,1)}, bf16[256,1280]{1,0:T(8,128)(2,1)}, bf16[256,256]{1,0:T(8,128)(2,1)}, bf16[256,256]{1,0:T(8,128)(2,1)}, bf16...) custom-call(bf16[128,2560]{1,0:T(8,128)(2,1)} %tok_ref.3, ...), custom_call_target="tpu_custom_call" | custom-call | flops 6710886400 | bytes 47185920 | tf_op jit(solution)/shard_map/pallas_call | solution.py:1214
  205.4 115.3 %shard_map.196 = (f32[128,2560]{1,0:T(8,128)}, f32[8,640]{1,0:T(8,128)}, bf16[4,2,2560,128]{3,2,1,0:T(8,128)(2,1)}, bf16[3,4,2,160,1024]{4,3,2,1,0:T(8,128)(2,1)}, bf16[128,2560]{1,0:T(8,128)(2,1)}) custom-call(f32[8,2560]{1,0:T(8,128)} %get-tuple-element.44.gain_ref, bf16[256,2560]{1,0:T(8,128)(2,1)} %get-tuple-element.45.own_hbm, ...), custom_call_target="tpu_custom_call" | custom-call | flops 48318382080 | bytes 62914560 | tf_op jit(solution)/shard_map/pallas_call | solution.py:524
  320.7 170.1 %shard_map.197 = (bf16[128,2560]{1,0:T(8,128)(2,1)}, bf16[128,2560]{1,0:T(8,128)(2,1)}, f32[8,640]{1,0:T(8,128)}, f32[80,512]{1,0:T(8,128)}, f32[160,1280]{1,0:T...) custom-call(bf16[128,2560]{1,0:T(8,128)(2,1)} %tok_ref.3, f32[8,2560]{1,0:T(8,128)} %get-tuple-element.44.gain_ref, ...), custom_call_target="tpu_custom_call" | custom-call | flops 11744051200 | bytes 32768000 | tf_op jit(solution)/shard_map/pallas_call | solution.py:1929
  490.8 0.0 copy-start
  490.8 6.5 %shard_map.198 = (f32[160,3840]{1,0:T(8,128)}, f32[160,3840]{1,0:T(8,128)}, f32[160,3840]{1,0:T(8,128)}, f32[160,1280]{1,0:T(8,128)}, f32[160,1280]{1,0:T(8,128)...) custom-call(bf16[3,4,2,160,1024]{4,3,2,1,0:T(8,128)(2,1)} %get-tuple-element.49.sums_hbm.sum_ref, ...), custom_call_target="tpu_custom_call" | custom-call | tf_op jit(solution)/shard_map/pallas_call | solution.py:2076
  497.3 0.0 copy-done
  497.3 0.1 constant_dynamic-slice_fusion
  497.4 0.5 slice_bitcast_fusion
  (2 shorter events, 0.0 us)
Async XLA Ops:
  490.8 6.5 %copy-start = (f32[8,640]{1,0:T(8,128)S(1)}, f32[8,640]{1,0:T(8,128)}, u32[]{:S(2)}) copy-start(f32[8,640]{1,0:T(8,128)} %get-tuple-element.71) | copy-start | bytes 61444

commit v2 on v0

--- a/solution.py
+++ b/solution.py
@@ -2065,13 +2065,13 @@
     z_size = lax.axis_size("z")
     main, units = ragged_split(ffn_cols, z_size)
     rows, cols = query_grad.shape
-    parts = rows // 32
+    parts = rows // 80
     kv_rows = kv_grad.shape[0] // parts
     full = lambda *dims: jax.ShapeDtypeStruct(dims, jnp.float32)
     row = lambda height, width: pl.BlockSpec((height, width), lambda index: (index, 0))
     own, width = mixed.shape
     share = pl.BlockSpec((own, width // parts), lambda index: (0, index))
-    specs = [row(32, cols), row(32, cols), row(kv_rows, kv_grad.shape[1]), share, share]
+    specs = [row(80, cols), row(80, cols), row(kv_rows, kv_grad.shape[1]), share, share]
     return pl.pallas_call(
         functools.partial(layout_kernel, z_size, main),
         grid=(parts,),
@@ -2084,11 +2084,11 @@
             jax.ShapeDtypeStruct(mixed.shape, jnp.bfloat16),
         ),
         in_specs=[
-            pl.BlockSpec((3, 1, 1, 32, units), lambda index: (0, 0, 0, index, 0)),
-            pl.BlockSpec((3, z_size, 32, units), lambda index: (0, 0, index, 0)),
+            pl.BlockSpec((3, 1, 1, 80, units), lambda index: (0, 0, 0, index, 0)),
+            pl.BlockSpec((3, z_size, 80, units), lambda index: (0, 0, index, 0)),
             *specs,
         ],
-        out_specs=(*[row(32, ffn_cols)] * 3, *specs),
+        out_specs=(*[row(80, ffn_cols)] * 3, *specs),
         compiler_params=pltpu.CompilerParams(vmem_limit_bytes=VMEM_BYTES),
     )(ffn_sums, ffn_grads, query_grad, out_grad, kv_grad, mixed, tokens_grad)
 

time: 500 us -> 498 us (level)
  no operation moved by 1% of the time
where the time goes in v2:
time: 498 us; the launch traced here: 491 us
  Pallas kernels  488 us (98%)
    pallas_call x1, Pallas kernels, pre_call(): pl.pallas_call(functools.partial(pre_kernel, z_size), out_shape=(low(seq,...  199 us
    pallas_call x1, Pallas kernels, post_call(): pl.pallas_call(functools.partial(post_kernel, z_size, main), out_shape=(o...  170 us
    pallas_call x1, Pallas kernels, ffn_call(): pl.pallas_call(functools.partial(ffn_kernel, z_size, main), out_shape=(ja...  112 us

profile of v2, /device:TPU:0, one launch (start us, length us, event | category | flops | bytes accessed | tf_op | source)
XLA Modules:
  0.0 491.3 jit_solution(12402157657547531790)
XLA Ops:
  0.7 0.7 convert_element_type.10
  1.3 1.2 fusion
  2.6 198.9 %shard_map.195 = (bf16[256,2560]{1,0:T(8,128)(2,1)}, bf16[256,1280]{1,0:T(8,128)(2,1)}, bf16[256,256]{1,0:T(8,128)(2,1)}, bf16[256,256]{1,0:T(8,128)(2,1)}, bf16...) custom-call(bf16[128,2560]{1,0:T(8,128)(2,1)} %tok_ref.3, ...), custom_call_target="tpu_custom_call" | custom-call | flops 6710886400 | bytes 47185920 | tf_op jit(solution)/shard_map/pallas_call | solution.py:1213
  201.5 112.0 %shard_map.196 = (f32[128,2560]{1,0:T(8,128)}, f32[8,640]{1,0:T(8,128)}, bf16[4,2,2560,128]{3,2,1,0:T(8,128)(2,1)}, bf16[3,4,2,160,1024]{4,3,2,1,0:T(8,128)(2,1)}, bf16[128,2560]{1,0:T(8,128)(2,1)}) custom-call(f32[8,2560]{1,0:T(8,128)} %get-tuple-element.44.gain_ref, bf16[256,2560]{1,0:T(8,128)(2,1)} %get-tuple-element.45.own_hbm, ...), custom_call_target="tpu_custom_call" | custom-call | flops 48318382080 | bytes 62914560 | tf_op jit(solution)/shard_map/pallas_call | solution.py:524
  313.5 170.2 %shard_map.197 = (bf16[128,2560]{1,0:T(8,128)(2,1)}, bf16[128,2560]{1,0:T(8,128)(2,1)}, f32[8,640]{1,0:T(8,128)}, f32[80,512]{1,0:T(8,128)}, f32[160,1280]{1,0:T...) custom-call(bf16[128,2560]{1,0:T(8,128)(2,1)} %tok_ref.3, f32[8,2560]{1,0:T(8,128)} %get-tuple-element.44.gain_ref, ...), custom_call_target="tpu_custom_call" | custom-call | flops 11744051200 | bytes 32768000 | tf_op jit(solution)/shard_map/pallas_call | solution.py:1928
  483.7 0.0 copy-start
  483.7 6.5 %shard_map.198 = (f32[160,3840]{1,0:T(8,128)}, f32[160,3840]{1,0:T(8,128)}, f32[160,3840]{1,0:T(8,128)}, f32[160,1280]{1,0:T(8,128)}, f32[160,1280]{1,0:T(8,128)...) custom-call(bf16[3,4,2,160,1024]{4,3,2,1,0:T(8,128)(2,1)} %get-tuple-element.49.sums_hbm.sum_ref, ...), custom_call_target="tpu_custom_call" | custom-call | tf_op jit(solution)/shard_map/pallas_call | solution.py:2075
  490.2 0.0 copy-done
  490.2 0.1 constant_dynamic-slice_fusion
  490.3 0.5 slice_bitcast_fusion
  (2 shorter events, 0.0 us)
Async XLA Ops:
  483.7 6.5 %copy-start = (f32[8,640]{1,0:T(8,128)S(1)}, f32[8,640]{1,0:T(8,128)}, u32[]{:S(2)}) copy-start(f32[8,640]{1,0:T(8,128)} %get-tuple-element.71) | copy-start | bytes 61444

commit v3 on v2

--- a/solution.py
+++ b/solution.py
@@ -1108,10 +1108,10 @@
 
     tasks = [
         lambda: (pass_cotangent(1), pass_if(inner, 2)),
-        lambda: hand_on(0, order[3]),
-        lambda: (cross(0, 0), hand_on(1, order[1])),
+        lambda: hand_on(1, order[1]),
+        lambda: (cross(0, 0), hand_on(1, order[2])),
         lambda: cross(1, 0),
-        lambda: (cross(2, 0), hand_on(1, order[2])),
+        lambda: (cross(2, 0), hand_on(0, order[3])),
     ]
     for index in range(heads):
         attend(index)

time: 498 us -> 498 us (level)
  no operation moved by 1% of the time
where the time goes in v3:
time: 498 us; the launch traced here: 491 us
  Pallas kernels  488 us (98%)
    pallas_call x1, Pallas kernels, pre_call(): pl.pallas_call(functools.partial(pre_kernel, z_size), out_shape=(low(seq,...  199 us
    pallas_call x1, Pallas kernels, post_call(): pl.pallas_call(functools.partial(post_kernel, z_size, main), out_shape=(o...  170 us
    pallas_call x1, Pallas kernels, ffn_call(): pl.pallas_call(functools.partial(ffn_kernel, z_size, main), out_shape=(ja...  112 us

profile of v3, /device:TPU:0, one launch (start us, length us, event | category | flops | bytes accessed | tf_op | source)
XLA Modules:
  0.0 491.3 jit_solution(14880708913124175337)
XLA Ops:
  0.7 0.7 convert_element_type.10
  1.3 1.2 fusion
  2.6 198.9 %shard_map.195 = (bf16[256,2560]{1,0:T(8,128)(2,1)}, bf16[256,1280]{1,0:T(8,128)(2,1)}, bf16[256,256]{1,0:T(8,128)(2,1)}, bf16[256,256]{1,0:T(8,128)(2,1)}, bf16...) custom-call(bf16[128,2560]{1,0:T(8,128)(2,1)} %tok_ref.3, ...), custom_call_target="tpu_custom_call" | custom-call | flops 6710886400 | bytes 47185920 | tf_op jit(solution)/shard_map/pallas_call | solution.py:1213
  201.5 112.0 %shard_map.196 = (f32[128,2560]{1,0:T(8,128)}, f32[8,640]{1,0:T(8,128)}, bf16[4,2,2560,128]{3,2,1,0:T(8,128)(2,1)}, bf16[3,4,2,160,1024]{4,3,2,1,0:T(8,128)(2,1)}, bf16[128,2560]{1,0:T(8,128)(2,1)}) custom-call(f32[8,2560]{1,0:T(8,128)} %get-tuple-element.44.gain_ref, bf16[256,2560]{1,0:T(8,128)(2,1)} %get-tuple-element.45.own_hbm, ...), custom_call_target="tpu_custom_call" | custom-call | flops 48318382080 | bytes 62914560 | tf_op jit(solution)/shard_map/pallas_call | solution.py:524
  313.5 170.2 %shard_map.197 = (bf16[128,2560]{1,0:T(8,128)(2,1)}, bf16[128,2560]{1,0:T(8,128)(2,1)}, f32[8,640]{1,0:T(8,128)}, f32[80,512]{1,0:T(8,128)}, f32[160,1280]{1,0:T...) custom-call(bf16[128,2560]{1,0:T(8,128)(2,1)} %tok_ref.3, f32[8,2560]{1,0:T(8,128)} %get-tuple-element.44.gain_ref, ...), custom_call_target="tpu_custom_call" | custom-call | flops 11744051200 | bytes 32768000 | tf_op jit(solution)/shard_map/pallas_call | solution.py:1928
  483.7 0.0 copy-start
  483.7 6.5 %shard_map.198 = (f32[160,3840]{1,0:T(8,128)}, f32[160,3840]{1,0:T(8,128)}, f32[160,3840]{1,0:T(8,128)}, f32[160,1280]{1,0:T(8,128)}, f32[160,1280]{1,0:T(8,128)...) custom-call(bf16[3,4,2,160,1024]{4,3,2,1,0:T(8,128)(2,1)} %get-tuple-element.49.sums_hbm.sum_ref, ...), custom_call_target="tpu_custom_call" | custom-call | tf_op jit(solution)/shard_map/pallas_call | solution.py:2075
  490.2 0.0 copy-done
  490.2 0.1 constant_dynamic-slice_fusion
  490.3 0.5 slice_bitcast_fusion
  (2 shorter events, 0.0 us)
Async XLA Ops:
  483.7 6.5 %copy-start = (f32[8,640]{1,0:T(8,128)S(1)}, f32[8,640]{1,0:T(8,128)}, u32[]{:S(2)}) copy-start(f32[8,640]{1,0:T(8,128)} %get-tuple-element.71) | copy-start | bytes 61444
